TPU v7x, 128 devices: a whole 4x4x4 slice. The times are simulated.
128 devices in a mesh: row: 16 (over y, z_lo, core), col: 8 (over x, z_hi).
Axes of the slice: x: 4, y: 4, z: 4 (z_hi: 2, z_lo: 2; z = z_hi * 2 + z_lo), core: 2. Of those that a mesh axis runs over, the one named last changes fastest.
Arguments:
- queries: bfloat16 [16, 96, 48, 1536], P(None, 'row', 'col')
- keys: bfloat16 [16, 96, 48, 1536], P(None, 'row', 'col')
- values: bfloat16 [16, 96, 48, 1536], P(None, 'row', 'col'), may hold values from -6 to 6
- tokens: bfloat16 [16, 96, 48, 3072], P(None, 'row', 'col'), may hold values from -6 to 6
- out_weight: bfloat16 [1536, 3072], replicated, may hold values from -0.15625 to 0.15625
- proj_weight: bfloat16 [3072, 512], replicated, may hold values from -0.109375 to 0.109375
- conv_weight: bfloat16 [13824, 512], P('row'), may hold values from -0.0546875 to 0.0546875
Outputs:
- upsampled: bfloat16 [16, 192, 96, 128], P('row', 'col')
All inputs are finite; a program needn't handle non-finite values.
Results may differ from a plain program's by a relative error of at most 0.0058.
Values may be sent and summed in bfloat16 or wider, within the bound.
A program may use at most 192 MiB of HBM per device.

v0:
```python
import math

import jax
import jax.numpy as jnp
from jax import lax
from jax.sharding import PartitionSpec as P

HEADS = 12


def shifted(block, axis, distance):
    devices = range(lax.axis_size(axis))
    route = [(i - distance, i) for i in devices if i - distance in devices]
    return lax.ppermute(block, axis, route)


def shifted_2(value, axis, by):
    devices = lax.axis_size(axis)
    return lax.ppermute(value, axis, [(i, (i + by) % devices) for i in range(devices)])


def attend_window(query_rows, key_rows, value_rows):
    count = query_rows.shape[0]
    inner = query_rows.shape[1]
    head_size = inner // HEADS
    query_heads = query_rows.reshape(count, HEADS, head_size)
    key_heads = key_rows.reshape(count, HEADS, head_size)
    value_heads = value_rows.reshape(count, HEADS, head_size)
    scores = jnp.einsum(
        "qhd,khd->hqk", query_heads, key_heads, preferred_element_type=jnp.float32
    ) / math.sqrt(head_size)
    highest = jnp.max(scores, axis=-1, keepdims=True)
    weights = jnp.exp(scores - highest)
    probs = (weights / jnp.sum(weights, axis=-1, keepdims=True)).astype(jnp.bfloat16)
    mixed = jnp.einsum("hqk,khd->qhd", probs, value_heads, preferred_element_type=jnp.float32)
    return mixed.astype(jnp.bfloat16).reshape(count, inner)


def earlier(field):
    return shifted(field, "row", 1)


def local(queries, keys, values, tokens, out_weight, proj_weight, conv_weight):
    frames = tokens.shape[0]
    tile = tokens.shape[1]
    half_cells = tile // 2
    cells = frames * tile * tile
    owned = (queries, keys, values, tokens)
    lower = shifted_2(
        (
            queries[:, :half_cells],
            keys[:, :half_cells],
            values[:, :half_cells],
            tokens[:, :half_cells],
        ),
        "row",
        -1,
    )
    taller = [
        jnp.concatenate([current[:, half_cells:], incoming], axis=1)
        for current, incoming in zip(owned, lower)
    ]
    beside = shifted_2(
        (
            taller[0][:, :, :half_cells],
            taller[1][:, :, :half_cells],
            taller[2][:, :, :half_cells],
            taller[3][:, :, :half_cells],
        ),
        "col",
        -1,
    )
    window = [
        jnp.concatenate([current[:, :, half_cells:], incoming], axis=2).reshape(
            cells, current.shape[-1]
        )
        for current, incoming in zip(taller, beside)
    ]
    attended = attend_window(window[0], window[1], window[2])
    residual = window[3] + jnp.dot(attended, out_weight, preferred_element_type=jnp.float32)
    normed = (
        residual * lax.rsqrt(jnp.mean(residual * residual, axis=-1, keepdims=True) + 1e-06)
    ).astype(jnp.bfloat16)
    features = jax.nn.silu(jnp.dot(normed, proj_weight, preferred_element_type=jnp.float32)).astype(
        jnp.bfloat16
    )
    channels = proj_weight.shape[1]
    row_count = lax.axis_size("row")
    col_count = lax.axis_size("col")
    group = row_count // col_count
    band_rows = group * tile
    breadth = col_count * tile
    blocks = features.reshape(frames, 1, tile, tile, channels)
    arrived = lax.all_to_all(
        lax.all_to_all(blocks, "row", split_axis=0, concat_axis=1, tiled=True),
        "col",
        split_axis=1,
        concat_axis=3,
        tiled=True,
    )
    band = arrived.reshape(band_rows, breadth, channels)
    band = jnp.roll(band, half_cells, axis=1)
    rim = shifted_2(band[band_rows - half_cells - 1 :], "col", 1)
    extended = jnp.concatenate([rim, band[: band_rows - half_cells + 1]], axis=0)
    position = jnp.arange(band_rows + 2)
    which_band = lax.axis_index("col")
    outside = jnp.logical_or(
        jnp.logical_and(position == 0, which_band == 0),
        jnp.logical_and(position == band_rows + 1, which_band == col_count - 1),
    )
    extended = jnp.where(outside[:, None, None], jnp.zeros_like(extended), extended)
    previous = earlier(extended)
    before_previous = earlier(previous)
    stacked = jnp.stack([before_previous, previous, extended])
    padded = jnp.pad(stacked, ((0, 0), (0, 0), (1, 1), (0, 0)))
    gathered = lax.all_gather(conv_weight, "row", axis=0, tiled=True)
    tapped = (
        gathered.reshape(9, 3, channels, channels)
        .transpose(0, 2, 1, 3)
        .reshape(9, channels, 3 * channels)
    )
    wide = breadth + 2
    running = jnp.zeros((band_rows * wide, 3 * channels), jnp.float32)
    for step_t in range(3):
        for off_y in range(3):
            slab = padded[step_t, off_y : off_y + band_rows].reshape(band_rows * wide, channels)
            running = running + jnp.dot(
                slab, tapped[step_t * 3 + off_y], preferred_element_type=jnp.float32
            )
    running = running.reshape(band_rows, wide, 3 * channels)
    summed = (
        running[:, 0:breadth, 0:channels]
        + running[:, 1 : breadth + 1, channels : 2 * channels]
        + running[:, 2 : breadth + 2, 2 * channels : 3 * channels]
    )
    conv_out = summed.reshape(band_rows * breadth, channels)
    shuffled = (
        conv_out.reshape(band_rows, breadth, channels // 4, 2, 2)
        .transpose(0, 3, 1, 4, 2)
        .reshape(2 * band_rows, 2 * breadth, channels // 4)
    )
    return shuffled.astype(jnp.bfloat16)[None]


def solution(mesh):
    placed = (
        P(None, "row", "col", None),
        P(None, "row", "col", None),
        P(None, "row", "col", None),
        P(None, "row", "col", None),
        P(),
        P(),
        P("row", None),
    )
    return jax.shard_map(
        local, mesh=mesh, in_specs=placed, out_specs=P("row", "col", None, None), check_vma=False
    )
```

profile of v0, /device:TPU:8, one launch (start us, length us, event | category | flops | bytes accessed | tf_op | source)
XLA Modules:
  0.0 474.8 jit_solution(10100509918422287715)
XLA Ops:
  15.5 6.3 %collective-permute-done.4 = bf16[16,3,6,1536]{3,0,2,1:T(8,128)(2,1)S(1)} collective-permute-done((bf16[16,3,6,1536]{3,0,2,1:T(8,128)(2,1)S(1)}, bf16[16,3,6,1536]{3,0,2,1:T(8,128)(2,1)S(1)}, u32[]{:S(2)}, u32[]{:S(2)}) %collective-permute-start.4) | collective-permute-done | bytes 884768 | tf_op jit(solution)/shard_map/ppermute | solution.py:19
  22.0 6.8 %collective-permute-start.5 = (bf16[16,6,3,1536]{3,0,2,1:T(8,128)(2,1)S(1)}, bf16[16,6,3,1536]{3,0,2,1:T(8,128)(2,1)S(1)}, u32[]{:S(2)}, u32[]{:S(2)}) collective-permute-start(bf16[16,6,3,1536]{3,0,2,1:T(8,128)(2,1)S(1)} %get-tuple-element.37), channel_id=1, source_target_pairs={{0,7},{1,0},{2,1},{3,2},{4,3},{5,4},{6,5},{7,6},{8,15},{9,8},{10,9... | collective-permute-start | bytes 2654216 | tf_op jit(solution)/shard_map/ppermute | solution.py:19
  28.8 21.4 %collective-permute-done.6 = bf16[16,3,6,1536]{3,0,2,1:T(8,128)(2,1)S(1)} collective-permute-done((bf16[16,3,6,1536]{3,0,2,1:T(8,128)(2,1)S(1)}, bf16[16,3,6,1536]{3,0,2,1:T(8,128)(2,1)S(1)}, u32[]{:S(2)}, u32[]{:S(2)}) %collective-permute-start.6) | collective-permute-done | bytes 884768 | tf_op jit(solution)/shard_map/ppermute | solution.py:19
  51.7 6.8 %collective-permute-start.7 = (bf16[16,6,3,1536]{3,0,2,1:T(8,128)(2,1)}, bf16[16,6,3,1536]{3,0,2,1:T(8,128)(2,1)}, u32[]{:S(2)}, u32[]{:S(2)}) collective-permute-start(bf16[16,6,3,1536]{3,0,2,1:T(8,128)(2,1)} %get-tuple-element.41), channel_id=1, source_target_pairs={{0,7},{1,0},{2,1},{3,2},{4,3},{5,4},{6,5},{7,6},{8,15},{9,8},{10,9... | collective-permute-start | bytes 2654216 | tf_op jit(solution)/shard_map/ppermute | solution.py:19
  58.4 15.1 %collective-permute-done.2 = bf16[16,3,6,1536]{3,0,2,1:T(8,128)(2,1)S(1)} collective-permute-done((bf16[16,3,6,1536]{3,0,2,1:T(8,128)(2,1)S(1)}, bf16[16,3,6,1536]{3,0,2,1:T(8,128)(2,1)S(1)}, u32[]{:S(2)}, u32[]{:S(2)}) %collective-permute-start.2) | collective-permute-done | bytes 884768 | tf_op jit(solution)/shard_map/ppermute | solution.py:19
  75.0 10.1 %collective-permute-start.3 = (bf16[16,6,3,1536]{3,0,2,1:T(8,128)(2,1)}, bf16[16,6,3,1536]{3,0,2,1:T(8,128)(2,1)}, u32[]{:S(2)}, u32[]{:S(2)}) collective-permute-start(bf16[16,6,3,1536]{3,0,2,1:T(8,128)(2,1)} %get-tuple-element.33), channel_id=1, source_target_pairs={{0,7},{1,0},{2,1},{3,2},{4,3},{5,4},{6,5},{7,6},{8,15},{9,8},{10,9... | collective-permute-start | bytes 2654216 | tf_op jit(solution)/shard_map/ppermute | solution.py:19
  87.7 5.2 %reshape_reshape.11 = bf16[576,12,128]{2,1,0:T(8,128)(2,1)} reshape(bf16[16,6,6,1536]{3,2,1,0:T(8,128)(2,1)} %copy.49) | data formatting | bytes 3538944 | tf_op jit(solution)/shard_map/reshape;reshape | solution.py:26
  92.9 12.0 %collective-permute-done.7 = bf16[16,6,3,1536]{3,0,2,1:T(8,128)(2,1)} collective-permute-done((bf16[16,6,3,1536]{3,0,2,1:T(8,128)(2,1)}, bf16[16,6,3,1536]{3,0,2,1:T(8,128)(2,1)}, u32[]{:S(2)}, u32[]{:S(2)}) %collective-permute-start.7) | collective-permute-done | bytes 884768 | tf_op jit(solution)/shard_map/ppermute | solution.py:19
  114.2 8.7 %collective-permute-done.3 = bf16[16,6,3,1536]{3,0,2,1:T(8,128)(2,1)} collective-permute-done((bf16[16,6,3,1536]{3,0,2,1:T(8,128)(2,1)}, bf16[16,6,3,1536]{3,0,2,1:T(8,128)(2,1)}, u32[]{:S(2)}, u32[]{:S(2)}) %collective-permute-start.3) | collective-permute-done | bytes 884768 | tf_op jit(solution)/shard_map/ppermute | solution.py:19
  138.2 15.0 %fusion.42 = (f32[12,576]{1,0:T(8,128)S(1)}, f32[12,576,576]{1,2,0:T(8,128)}) fusion(bf16[576,12,128]{2,1,0:T(8,128)(2,1)} %reshape_reshape.12, bf16[576,12,128]{2,1,0:T(8,128)(2,1)} %reshape_reshape.11), kind=kOutput, calls=%fused_computation.65 | convolution fusion | flops 1031160384 | bytes 19491840 | tf_op jit(solution)/shard_map/sub | solution.py:33
  153.2 11.2 %convert_bitcast_fusion = bf16[576,12,128]{2,0,1:T(8,128)(2,1)} fusion(f32[12,576,576]{1,2,0:T(8,128)} %get-tuple-element.45, f32[12,576]{1,0:T(8,128)S(1)} %get-tuple-element.44, bf16[576,12,128]{2,1,0:T(8,128)(2,1)} %reshape_reshape.10), kind=kOutput, calls=%fused_computation.37 | convolution fusion | flops 1028063232 | bytes 19491840 | tf_op jit(solution)/shard_map/hqk,khd->qhd/dot_general | solution.py:35
  168.7 11.0 %fusion.51 = f32[576,3072]{1,0:T(8,128)} fusion(bf16[576,1536]{0,1:T(8,128)(2,1)} %bitcast.62, bf16[1536,3072]{1,0:T(8,128)(2,1)} %param.11), kind=kOutput, calls=%fused_computation.66 | convolution fusion | flops 5435817984 | bytes 18284544 | tf_op jit(solution)/shard_map/dot_general | solution.py:80
  181.6 7.9 %copy.47 = f32[16,6,6,3072]{3,2,1,0:T(8,128)} copy(f32[16,6,6,3072]{3,0,2,1:T(8,128)S(1)} %maximum_convert_fusion) | data formatting | bytes 14155776 | tf_op jit(solution)/shard_map/convert_element_type | solution.py:80
  189.5 8.1 %reshape.107 = f32[576,3072]{1,0:T(8,128)} reshape(f32[16,6,6,3072]{3,2,1,0:T(8,128)} %copy.47) | data formatting | bytes 14155776 | tf_op jit(solution)/shard_map/convert_element_type | solution.py:80
  197.6 5.9 %multiply_reduce_fusion.1 = (f32[576]{0:T(1024)S(1)}, f32[576,3072]{1,0:T(8,128)S(1)}) fusion(f32[576,3072]{1,0:T(8,128)} %reshape.107, f32[576,3072]{1,0:T(8,128)} %fusion.51), kind=kLoop, calls=%fused_computation.10 | loop fusion | flops 5307840 | bytes 21235968 | tf_op jit(solution)/shard_map/reduce_sum | solution.py:82
  207.8 97.4 %all_to_all.27 = bf16[16,1,6,6,512]{4,3,2,1,0:T(8,128)(2,1)} all-to-all(bf16[16,1,6,6,512]{4,3,2,1,0:T(8,128)(2,1)S(1)} %bitcast.60), channel_id=1, replica_groups=mesh['row'=16,'col'=8] {'row'}, dimensions={0} | all-to-all | bytes 1179648 | tf_op jit(solution)/shard_map/all_to_all | solution.py:95
  305.2 6.1 %all-to-all-start.1 = ((bf16[1,16,6,6,512]{4,3,2,0,1:T(8,128)(2,1)}), bf16[1,16,6,6,512]{4,3,2,0,1:T(8,128)(2,1)S(1)}, u32[]{:S(2)}, u32[]{:S(2)}) async-start(bf16[1,16,6,6,512]{4,3,2,0,1:T(8,128)(2,1)} %bitcast.4), calls=%async_computation.1 | async-start | bytes 1572864 | tf_op jit(solution)/shard_map/all_to_all | solution.py:94
  311.3 14.0 %all-to-all-done.1 = bf16[1,16,6,6,512]{4,3,2,0,1:T(8,128)(2,1)S(1)} async-done(((bf16[1,16,6,6,512]{4,3,2,0,1:T(8,128)(2,1)}), bf16[1,16,6,6,512]{4,3,2,0,1:T(8,128)(2,1)S(1)}, u32[]{:S(2)}, u32[]{:S(2)}) %all-to-all-start.1) | async-done | bytes 589856 | tf_op jit(solution)/shard_map/all_to_all | solution.py:94
  328.2 7.5 %collective-permute-done.8 = bf16[4,48,512]{2,1,0:T(8,128)(2,1)S(1)} collective-permute-done((bf16[4,48,512]{2,1,0:T(8,128)(2,1)S(1)}, bf16[4,48,512]{2,1,0:T(8,128)(2,1)S(1)}, u32[]{:S(2)}, u32[]{:S(2)}) %collective-permute-start.8) | collective-permute-done | bytes 196640 | tf_op jit(solution)/shard_map/ppermute | solution.py:19
  337.9 11.1 %collective-permute-done.9 = bf16[14,48,512]{2,1,0:T(8,128)(2,1)S(1)} collective-permute-done((bf16[14,48,512]{2,1,0:T(8,128)(2,1)S(1)}, bf16[14,48,512]{2,1,0:T(8,128)(2,1)S(1)}, u32[]{:S(2)}, u32[]{:S(2)}) %collective-permute-start.9) | collective-permute-done | bytes 688160 | tf_op jit(solution)/shard_map/ppermute | solution.py:14
  351.1 11.1 %collective-permute-done.10 = bf16[14,48,512]{2,1,0:T(8,128)(2,1)S(1)} collective-permute-done((bf16[14,48,512]{2,1,0:T(8,128)(2,1)S(1)}, bf16[14,48,512]{2,1,0:T(8,128)(2,1)S(1)}, u32[]{:S(2)}, u32[]{:S(2)}) %collective-permute-start.10) | collective-permute-done | bytes 688160 | tf_op jit(solution)/shard_map/ppermute | solution.py:14
  379.4 9.0 %fusion.35 = (bf16[1,512,3,512]{3,1,2,0:T(8,128)(2,1)S(1)}, bf16[1,512,3,512]{3,1,2,0:T(8,128)(2,1)S(1)}, bf16[1,512,3,512]{3,1,2,0:T(8,128)(2,1)}, bf16[1,512,3...) fusion(bf16[9,512,3,512]{3,1,2,0:T(8,128)(2,1)} %bitcast.53), kind=kLoop, calls=%fused_computation.58 | loop fusion | bytes 28311552 | tf_op jit(solution)/shard_map/slice | solution.py:128
  430.0 10.8 %add_add_fusion = f32[600,1536]{1,0:T(8,128)} fusion(f32[600,1536]{1,0:T(8,128)} %fusion.59, f32[600,1536]{1,0:T(8,128)} %fusion.58, f32[600,1536]{1,0:T(8,128)} %fusion.57, f32[600,1536]{1,0:T(8,128)} %fusion.56, f32[600,1536]{1,0:T(8,128)} %fusion.55, f32[600,1536]{1,0:T(8,128)S(1)} %fusion.54, f32[600,1536]{1,0:T(8,128)S(1)} %fusion.52, ...), kind=kOutput, calls=%fused_computation.12 | convolution fusion | flops 951091200 | bytes 35364864 | tf_op jit(solution)/shard_map/dot_general | solution.py:127
  457.3 5.5 %add_convert_fusion = bf16[12,48,512]{1,2,0:T(8,128)(2,1)} fusion(f32[12,48,512]{1,2,0:T(8,128)} %copy.75, f32[12,48,512]{1,2,0:T(8,128)} %copy.73, f32[12,48,512]{1,2,0:T(8,128)} %copy.74), kind=kLoop, calls=%fused_computation.18 | loop fusion | flops 884736 | bytes 4128768 | tf_op jit(solution)/shard_map/convert_element_type | solution.py:142
  (127 shorter events, 136.7 us)
Async XLA Ops:
  6.5 197.0 %copy-start = (bf16[3072,512]{1,0:T(8,128)(2,1)S(1)}, bf16[3072,512]{1,0:T(8,128)(2,1)}, u32[]{:S(2)}) copy-start(bf16[3072,512]{1,0:T(8,128)(2,1)} %param.12) | copy-start | bytes 9437188
  6.5 372.8 %all-gather.2.cloned.1.call-start = ((), (), s32[]{:S(2)}) async-start(), calls=%async_computation.2 | async-start | bytes 15040512 | tf_op jit(solution)/shard_map/all_gather | solution.py:116
  7.3 3.2 copy-start.9
  9.1 12.7 %collective-permute-start.4 = (bf16[16,3,6,1536]{3,0,2,1:T(8,128)(2,1)S(1)}, bf16[16,3,6,1536]{3,0,2,1:T(8,128)(2,1)S(1)}, u32[]{:S(2)}, u32[]{:S(2)}) collective-permute-start(bf16[16,3,6,1536]{3,0,2,1:T(8,128)(2,1)S(1)} %get-tuple-element.39), channel_id=1, source_target_pairs={{0,120},{8,0},{16,8},{24,16},{32,24},{40,32},{48,40},{56,48},{64,5... | collective-permute-start | bytes 2654216 | tf_op jit(solution)/shard_map/ppermute | solution.py:19
  10.6 39.7 %collective-permute-start.6 = (bf16[16,3,6,1536]{3,0,2,1:T(8,128)(2,1)S(1)}, bf16[16,3,6,1536]{3,0,2,1:T(8,128)(2,1)S(1)}, u32[]{:S(2)}, u32[]{:S(2)}) collective-permute-start(bf16[16,3,6,1536]{3,0,2,1:T(8,128)(2,1)S(1)} %get-tuple-element.43), channel_id=1, source_target_pairs={{0,120},{8,0},{16,8},{24,16},{32,24},{40,32},{48,40},{56,48},{64,5... | collective-permute-start | bytes 2654216 | tf_op jit(solution)/shard_map/ppermute | solution.py:19
  11.4 62.1 %collective-permute-start.2 = (bf16[16,3,6,1536]{3,0,2,1:T(8,128)(2,1)S(1)}, bf16[16,3,6,1536]{3,0,2,1:T(8,128)(2,1)S(1)}, u32[]{:S(2)}, u32[]{:S(2)}) collective-permute-start(bf16[16,3,6,1536]{3,0,2,1:T(8,128)(2,1)S(1)} %get-tuple-element.35), channel_id=1, source_target_pairs={{0,120},{8,0},{16,8},{24,16},{32,24},{40,32},{48,40},{56,48},{64,5... | collective-permute-start | bytes 2654216 | tf_op jit(solution)/shard_map/ppermute | solution.py:19
  14.8 117.4 %collective-permute-start = (bf16[16,3,6,3072]{3,0,2,1:T(8,128)(2,1)}, bf16[16,3,6,3072]{3,0,2,1:T(8,128)(2,1)}, u32[]{:S(2)}, u32[]{:S(2)}) collective-permute-start(bf16[16,3,6,3072]{3,0,2,1:T(8,128)(2,1)} %get-tuple-element.22), channel_id=1, source_target_pairs={{0,120},{8,0},{16,8},{24,16},{32,24},{40,32},{48,40},{56,48},{64,5... | collective-permute-start | bytes 5308424 | tf_op jit(solution)/shard_map/ppermute | solution.py:19
  22.0 63.1 %collective-permute-start.5 = (bf16[16,6,3,1536]{3,0,2,1:T(8,128)(2,1)S(1)}, bf16[16,6,3,1536]{3,0,2,1:T(8,128)(2,1)S(1)}, u32[]{:S(2)}, u32[]{:S(2)}) collective-permute-start(bf16[16,6,3,1536]{3,0,2,1:T(8,128)(2,1)S(1)} %get-tuple-element.37), channel_id=1, source_target_pairs={{0,7},{1,0},{2,1},{3,2},{4,3},{5,4},{6,5},{7,6},{8,15},{9,8},{10,9... | collective-permute-start | bytes 2654216 | tf_op jit(solution)/shard_map/ppermute | solution.py:19
  51.7 53.3 %collective-permute-start.7 = (bf16[16,6,3,1536]{3,0,2,1:T(8,128)(2,1)}, bf16[16,6,3,1536]{3,0,2,1:T(8,128)(2,1)}, u32[]{:S(2)}, u32[]{:S(2)}) collective-permute-start(bf16[16,6,3,1536]{3,0,2,1:T(8,128)(2,1)} %get-tuple-element.41), channel_id=1, source_target_pairs={{0,7},{1,0},{2,1},{3,2},{4,3},{5,4},{6,5},{7,6},{8,15},{9,8},{10,9... | collective-permute-start | bytes 2654216 | tf_op jit(solution)/shard_map/ppermute | solution.py:19
  75.0 47.9 %collective-permute-start.3 = (bf16[16,6,3,1536]{3,0,2,1:T(8,128)(2,1)}, bf16[16,6,3,1536]{3,0,2,1:T(8,128)(2,1)}, u32[]{:S(2)}, u32[]{:S(2)}) collective-permute-start(bf16[16,6,3,1536]{3,0,2,1:T(8,128)(2,1)} %get-tuple-element.33), channel_id=1, source_target_pairs={{0,7},{1,0},{2,1},{3,2},{4,3},{5,4},{6,5},{7,6},{8,15},{9,8},{10,9... | collective-permute-start | bytes 2654216 | tf_op jit(solution)/shard_map/ppermute | solution.py:19
  136.2 43.4 %collective-permute-start.1 = (bf16[16,6,3,3072]{3,0,2,1:T(8,128)(2,1)}, bf16[16,6,3,3072]{3,0,2,1:T(8,128)(2,1)}, u32[]{:S(2)}, u32[]{:S(2)}) collective-permute-start(bf16[16,6,3,3072]{3,0,2,1:T(8,128)(2,1)} %get-tuple-element.20), channel_id=1, source_target_pairs={{0,7},{1,0},{2,1},{3,2},{4,3},{5,4},{6,5},{7,6},{8,15},{9,8},{10,9... | collective-permute-start | bytes 5308424 | tf_op jit(solution)/shard_map/ppermute | solution.py:19
  168.7 11.0 %copy-start.2 = (bf16[16,6,3,3072]{3,0,2,1:T(8,128)(2,1)S(1)}, bf16[16,6,3,3072]{3,0,2,1:T(8,128)(2,1)}, u32[]{:S(2)}) copy-start(bf16[16,6,3,3072]{3,0,2,1:T(8,128)(2,1)} %get-tuple-element.19) | copy-start | bytes 5308420
  305.2 20.2 %all-to-all-start.1 = ((bf16[1,16,6,6,512]{4,3,2,0,1:T(8,128)(2,1)}), bf16[1,16,6,6,512]{4,3,2,0,1:T(8,128)(2,1)S(1)}, u32[]{:S(2)}, u32[]{:S(2)}) async-start(bf16[1,16,6,6,512]{4,3,2,0,1:T(8,128)(2,1)} %bitcast.4), calls=%async_computation.1 | async-start | bytes 1572864 | tf_op jit(solution)/shard_map/all_to_all | solution.py:94
  325.7 10.0 %collective-permute-start.8 = (bf16[4,48,512]{2,1,0:T(8,128)(2,1)S(1)}, bf16[4,48,512]{2,1,0:T(8,128)(2,1)S(1)}, u32[]{:S(2)}, u32[]{:S(2)}) collective-permute-start(bf16[4,48,512]{2,1,0:T(8,128)(2,1)S(1)} %pad_maximum_fusion.8), channel_id=1, source_target_pairs={{0,1},{1,2},{2,3},{3,4},{4,5},{5,6},{6,7},{7,0},{8,9},{9,10},{10,1... | collective-permute-start | bytes 589832 | tf_op jit(solution)/shard_map/ppermute | solution.py:19
  335.8 13.2 %collective-permute-start.9 = (bf16[14,48,512]{2,1,0:T(8,128)(2,1)S(1)}, bf16[14,48,512]{2,1,0:T(8,128)(2,1)S(1)}, u32[]{:S(2)}, u32[]{:S(2)}) collective-permute-start(bf16[14,48,512]{2,1,0:T(8,128)(2,1)S(1)} %maximum_select_fusion), channel_id=1, source_target_pairs={{0,8},{8,16},{16,24},{24,32},{32,40},{40,48},{48,56},{56,64},{64,7... | collective-permute-start | bytes 2064392 | tf_op jit(solution)/shard_map/ppermute | solution.py:14
  349.0 13.1 %collective-permute-start.10 = (bf16[14,48,512]{2,1,0:T(8,128)(2,1)S(1)}, bf16[14,48,512]{2,1,0:T(8,128)(2,1)S(1)}, u32[]{:S(2)}, u32[]{:S(2)}) collective-permute-start(bf16[14,48,512]{2,1,0:T(8,128)(2,1)S(1)} %collective-permute-done.9), channel_id=1, source_target_pairs={{0,8},{8,16},{16,24},{24,32},{32,40},{40,48},{48,56},{56,64},{64,7... | collective-permute-start | bytes 2064392 | tf_op jit(solution)/shard_map/ppermute | solution.py:14
  365.7 4.3 copy-start.7
  367.8 7.4 %copy-start.6 = (bf16[1,12,50,512]{3,2,1,0:T(8,128)(2,1)S(1)}, bf16[1,12,50,512]{3,2,1,0:T(8,128)(2,1)}, u32[]{:S(2)}) copy-start(bf16[1,12,50,512]{3,2,1,0:T(8,128)(2,1)} %get-tuple-element.26) | copy-start | bytes 1843204
  370.0 6.3 %copy-start.5 = (bf16[1,12,50,512]{3,2,1,0:T(8,128)(2,1)S(1)}, bf16[1,12,50,512]{3,2,1,0:T(8,128)(2,1)}, u32[]{:S(2)}) copy-start(bf16[1,12,50,512]{3,2,1,0:T(8,128)(2,1)} %get-tuple-element.25) | copy-start | bytes 1843204
  371.0 6.3 %copy-start.4 = (bf16[1,12,50,512]{3,2,1,0:T(8,128)(2,1)S(1)}, bf16[1,12,50,512]{3,2,1,0:T(8,128)(2,1)}, u32[]{:S(2)}) copy-start(bf16[1,12,50,512]{3,2,1,0:T(8,128)(2,1)} %get-tuple-element.24) | copy-start | bytes 1843204
  420.8 3.1 copy-start.12
  420.8 3.1 copy-start.19
  423.9 3.1 copy-start.18
  457.3 10.4 %copy-start.1 = (bf16[3072,512]{1,0:T(8,128)(2,1)S(1)}, bf16[3072,512]{1,0:T(8,128)(2,1)}, u32[]{:S(2)}) copy-start(bf16[3072,512]{1,0:T(8,128)(2,1)} %param.12) | copy-start | bytes 9437188
  (14 other events, 33.9 us)
Sparse Core Ops, SparseCore 0:
  9.1 189.5 all-gather.1
where the time goes:
time: 484 us; the launch traced here: 475 us
  local copies, waits for them, and re-layouts  117 us (24%)
  waiting for transfers between devices  108 us (22%)
  blocking collectives  97.4 us (20%)
  matrix products  71.3 us (15%)
  starting transfers between devices  41.6 us (9%)
  other arithmetic  25.3 us (5%)
  between operations  13.9 us (3%)
    all_to_all x1, blocking collectives, local(): lax.all_to_all(blocks, 'row', split_axis=0, concat_axis=1, tiled=True)  97.4 us
    ppermute x9, waiting for transfers between devices, shifted_2(): lax.ppermute(value, axis, [(i, (i + by) % devices) for i in range(devices)])  71.1 us
    ppermute x9, starting transfers between devices, shifted_2(): lax.ppermute(value, axis, [(i, (i + by) % devices) for i in range(devices)])  31.4 us
    dot_general x9, matrix products, local(): jnp.dot(slab, tapped[step_t * 3 + off_y], preferred_element_type=jnp.floa...  31.1 us
    slice x10, local copies, waits for them, and re-layouts, local(): tapped[step_t * 3 + off_y]  29.5 us
    ppermute x2, waiting for transfers between devices, shifted(): return lax.ppermute(block, axis, route)  22.1 us
    convert_element_type x2, local copies, waits for them, and re-layouts, local(): window[3]  16 us
    sub x1, matrix products, attend_window(): weights = jnp.exp(scores - highest)  15 us
  transfers between devices with their start and end apart: 13, of which 9 were waited for; matrix products, arithmetic and copies ran while one was open for 26% of the time, Pallas kernels for 0%

commit v1 on v0

v1 whole, which is shorter than its diff:
```python
import math

import jax
import jax.numpy as jnp
from jax import lax
from jax.experimental import pallas as pl
from jax.experimental.pallas import tpu as pltpu
from jax.sharding import PartitionSpec as P

MESH = pl.DeviceIdType.MESH
HEADS = 12
HEAD = 128
GROUPS = 6
WIDE = 256
INNER = 1536
D = 3072
CH = 512
SHARD = 864
HALF = 432
ROWS = 576
CHUNK = 512
F32 = jnp.float32
BF16 = jnp.bfloat16


def lanes(start, size):
    return pl.ds(pl.multiple_of(start, 128), size)


def body(q_ref, k_ref, v_ref, t_ref, wo_ref, wp_ref, cw_ref, out_ref,
         win, att, home, res, tok, wo, wp, cw, shard, field, acc, parts, perm, back, sent, got, ssq,
         fs, fr, rs, rr, ls, ws, wr, hs, hr, os_, or_):
    r = lax.axis_index("row")
    c = lax.axis_index("col")
    odd = lax.rem(r, 2)
    x, zh = lax.div(c, 2), lax.rem(c, 2)
    y, zl = lax.div(r, 4), lax.rem(lax.div(r, 2), 2)

    def at(row, col):
        return (lax.rem(row + 16, 16), lax.rem(col + 8, 8))

    def along_x(step):
        return (r, lax.rem(x + step, 4) * 2 + zh)

    def along_y(step):
        return (lax.rem(y + step, 4) * 4 + zl * 2 + odd, c)

    other_zl = (y * 4 + (1 - zl) * 2 + odd, c)
    other_core = (r + 1 - 2 * odd, c)
    forward = (at(r - 1, c - odd), at(r - 1, c + 1 - odd), at(r, c - 1 + 2 * odd))
    homes = (at(r + 1, c + 1 - odd), at(r + 1, c - odd), at(r, c + 1 - 2 * odd))
    around = [(dr, dc) for dr in (-1, 0, 1) for dc in (-1, 0, 1) if (dr, dc) != (0, 0)]
    own_band = lax.div(r, 2) == c

    barrier = pltpu.get_barrier_semaphore()

    def greet(device):
        pl.semaphore_signal(barrier, inc=1, device_id=device, device_id_type=MESH)

    for device in forward + homes:
        greet(device)
    for dr, dc in around:
        greet(at(r + dr, c + dc))
    for step in (1, 2, 3):
        greet(along_x(step))
        greet(along_y(step))
    greet(other_zl)
    greet(other_core)

    def greet_band(i, carry):
        row, col = 2 * c + lax.div(i, 8), lax.rem(i, 8)

        @pl.when(jnp.logical_or(row != r, col != c))
        def _():
            greet((row, col))

        return carry

    lax.fori_loop(0, 16, greet_band, 0)

    local = [
        pltpu.make_async_copy(cw_ref, shard, ls.at[0]),
        pltpu.make_async_copy(t_ref, tok, ls.at[1]),
        pltpu.make_async_copy(wo_ref, wo, ls.at[2]),
        pltpu.make_async_copy(wp_ref, wp, ls.at[3]),
    ]
    sources = (q_ref, k_ref, v_ref)
    for n in range(3):
        local.append(
            pltpu.make_async_copy(
                sources[n].at[pl.ds(3, 3), pl.ds(3 * (1 - odd), 3)], win.at[n, odd], ls.at[4 + n]
            )
        )
    local[0].start()
    for copy in local[4:]:
        copy.start()

    pl.semaphore_wait(barrier, 38 - own_band.astype(jnp.int32))

    def send(g, n, t):
        span = lanes(g * WIDE, WIDE)
        if t == 2:
            src = sources[n].at[pl.ds(3, 3), pl.ds(3 * odd, 3), :, span]
            dst = win.at[n, 1 - odd, :, :, :, span]
        else:
            src = sources[n].at[pl.ds(0, 3), pl.ds(3 * t, 3), :, span]
            dst = win.at[n, 3 - t, :, :, :, span]
        return pltpu.make_async_remote_copy(
            src_ref=src, dst_ref=dst, send_sem=fs.at[g, n, t], recv_sem=fr.at[g, n, t],
            device_id=forward[t], device_id_type=MESH,
        )

    def give(g, t):
        span = lanes(g * WIDE, WIDE)
        if t == 2:
            src = att.at[1 - odd, :, :, :, span]
            dst = home.at[pl.ds(3, 3), pl.ds(3 * odd, 3), :, span]
        else:
            src = att.at[3 - t, :, :, :, span]
            dst = home.at[pl.ds(0, 3), pl.ds(3 * t, 3), :, span]
        return pltpu.make_async_remote_copy(
            src_ref=src, dst_ref=dst, send_sem=rs.at[g, t], recv_sem=rr.at[g, t],
            device_id=homes[t], device_id_type=MESH,
        )

    def keep(g):
        span = lanes(g * WIDE, WIDE)
        return pltpu.make_async_copy(
            att.at[odd, :, :, :, span], home.at[pl.ds(3, 3), pl.ds(3 * (1 - odd), 3), :, span], rr.at[g, 3]
        )

    def send_group(g):
        for n in range(3):
            for t in (2, 0, 1):
                send(g, n, t).start()

    send_group(0)
    send_group(1)
    for copy in local[1:4]:
        copy.start()

    quarter = lanes(x * 128, 128)
    everything = pl.ds(0, CH)

    def piece(i, y_, zl_, part, span, device):
        first, size = part
        start = pl.multiple_of((y_ * 4 + zl_ * 2 + odd) * SHARD + first, 16)
        block = cw.at[pl.ds(start, size), span]
        return pltpu.make_async_remote_copy(
            src_ref=block, dst_ref=block, send_sem=ws.at[i], recv_sem=wr.at[i],
            device_id=device, device_id_type=MESH,
        )

    def whose_y(step):
        return lax.rem(y + step, 4)

    low, high, full = (0, HALF), (HALF, HALF), (0, SHARD)
    stage_0 = [(0, y, zl, full, quarter, other_zl)]
    for s in (1, 2, 3):
        stage_0.append((s, y, zl, low, quarter, along_y(s)))
        stage_0.append((3 + s, y, zl, high, everything, along_y(s)))
    stage_1 = []
    for s in (1, 2, 3):
        stage_1.append((6 + s, y, 1 - zl, low, quarter, along_y(s)))
        stage_1.append((9 + s, y, 1 - zl, high, quarter, along_x(s)))
        stage_1.append((12 + s, y, 1 - zl, low, quarter, along_x(s)))
        for d in (1, 2, 3):
            stage_1.append((12 + 3 * d + s, whose_y(d), zl, low, quarter, along_x(s)))
    stage_2 = []
    for s in (1, 2, 3):
        stage_2.append((24 + s, y, 1 - zl, high, everything, along_y(s)))
        for d in (1, 2, 3):
            stage_2.append((24 + 3 * d + s, whose_y(d), 1 - zl, low, quarter, along_x(s)))
    swap_0 = [(37, y, zl, full, everything, other_core)]
    swap_1 = [(37 + d, whose_y(d), zl, high, everything, other_core) for d in (1, 2, 3)]
    swap_2 = [(41, y, 1 - zl, full, everything, other_core)]
    swap_3 = []
    for d in (1, 2, 3):
        swap_3.append((41 + d, whose_y(d), zl, low, everything, other_core))
        swap_3.append((44 + d, whose_y(d), 1 - zl, full, everything, other_core))

    def start_all(pieces):
        for item in pieces:
            piece(*item).start()

    def wait_all(pieces, which=None):
        for item in pieces:
            if which is None or item[0] in which:
                piece(*item).wait_recv()

    def drain(pieces):
        for item in pieces:
            piece(*item).wait_send()

    local[0].wait()
    key = lax.broadcasted_iota(jnp.int32, (CH, CH), 0)
    lane = lax.broadcasted_iota(jnp.int32, (CH, CH), 1)
    order = jnp.where(key == 4 * (lane & 127) + (lane >> 7), 1.0, 0.0).astype(BF16)
    own_start = pl.multiple_of(r * SHARD, 16)
    for part in range(3):
        cw[pl.ds(own_start + 288 * part, 288), :] = jnp.dot(
            shard[pl.ds(288 * part, 288), :], order, preferred_element_type=F32
        ).astype(BF16)
    start_all(stage_0)
    start_all(swap_0)

    row = lax.broadcasted_iota(jnp.int32, (256, 192), 0)
    col = lax.broadcasted_iota(jnp.int32, (256, 192), 1)
    frame, place = row >> 4, row & 15
    wanted = (place & 1) * 96 + (place >> 1) * 16 + frame
    perm[...] = jnp.where(jnp.logical_and(place < 12, col == wanted), 1.0, 0.0).astype(BF16)
    row = lax.broadcasted_iota(jnp.int32, (96, 128), 0)
    col = lax.broadcasted_iota(jnp.int32, (96, 128), 1)
    which = (row * 171) >> 11
    back[...] = jnp.where(col == which * 16 + row - 12 * which, 1.0, 0.0).astype(BF16)

    for copy in local[4:]:
        copy.wait()

    def attend(h):
        span = lanes(h * HEAD, HEAD)
        keys = win[1, :, :, :, :, span].reshape(ROWS, HEAD)
        values = win[2, :, :, :, :, span].reshape(ROWS, HEAD)
        for part in range(2):
            queries = win[0, pl.ds(2 * part, 2), :, :, :, span].reshape(ROWS // 2, HEAD)
            scores = lax.dot_general(
                queries, keys, (((1,), (1,)), ((), ())), preferred_element_type=F32
            ) * (1.0 / math.sqrt(HEAD))
            highest = jnp.max(scores, axis=-1, keepdims=True)
            weights = jnp.exp(scores - highest)
            probs = (weights * (1.0 / jnp.sum(weights, axis=-1, keepdims=True))).astype(BF16)
            mixed = jnp.dot(probs, values, preferred_element_type=F32).astype(BF16)
            att[pl.ds(2 * part, 2), :, :, :, span] = mixed.reshape(2, 3, 3, 16, HEAD)

    def await_home(g):
        for t in range(3):
            give(g, t).wait_recv()
        keep(g).wait()

    def add_group(g, first):
        rows = home[:, :, :, lanes(g * WIDE, WIDE)].reshape(ROWS, WIDE)

        def chunk(n, carry):
            span = lanes(n * CHUNK, CHUNK)
            product = jnp.dot(
                rows, wo[pl.ds(pl.multiple_of(g * WIDE, WIDE), WIDE), span], preferred_element_type=F32
            )
            base = tok[:, span].astype(F32) if first else res[:, span]
            res[:, span] = base + product
            return carry

        lax.fori_loop(0, D // CHUNK, chunk, 0)

    def group(g, carry):
        for n in range(3):
            for t in range(3):
                send(g, n, t).wait_recv()

        @pl.when(g < GROUPS - 2)
        def _():
            for n in range(3):
                for t in range(3):
                    send(g, n, t).wait_send()
            send_group(g + 2)

        for h in range(WIDE // HEAD):
            attend(g * (WIDE // HEAD) + h)
        for t in (2, 0, 1):
            give(g, t).start()
        keep(g).start()

        @pl.when(g == 0)
        def _():
            wait_all(stage_0)
            start_all(stage_1)
            start_all(swap_1)
            for copy in local[1:4]:
                copy.wait()

        @pl.when(g == 2)
        def _():
            wait_all(stage_1, (7, 8, 9, 10, 11, 12, 13, 14, 15))
            start_all(stage_2)
            start_all(swap_2)

        @pl.when(g == 1)
        def _():
            await_home(0)
            add_group(0, True)

        @pl.when(g > 1)
        def _():
            await_home(g - 1)
            add_group(g - 1, False)

        return carry

    lax.fori_loop(0, GROUPS, group, 0)

    wait_all(stage_1, tuple(range(16, 25)))
    wait_all(stage_2)
    start_all(swap_3)

    last = GROUPS - 1
    await_home(last)
    rows = home[:, :, :, pl.ds(last * WIDE, WIDE)].reshape(ROWS, WIDE)
    ssq[...] = jnp.zeros_like(ssq)
    acc[...] = jnp.zeros_like(acc)

    def finish(n, carry):
        span = lanes(n * CHUNK, CHUNK)
        total = res[:, span] + jnp.dot(rows, wo[pl.ds(last * WIDE, WIDE), span], preferred_element_type=F32)
        ssq[...] += jnp.sum(total * total, axis=-1, keepdims=True)
        acc[...] += jnp.dot(
            total.astype(BF16), wp[pl.ds(pl.multiple_of(n * CHUNK, CHUNK), CHUNK), :], preferred_element_type=F32
        )
        return carry

    lax.fori_loop(0, D // CHUNK, finish, 0)
    raw = acc[...] * lax.rsqrt(ssq[...] * (1.0 / D) + 1e-6)
    features = (raw / (1.0 + jnp.exp(-raw))).astype(BF16)
    field[pl.ds(1, 6), pl.ds(1, 6)] = features.reshape(6, 6, 16, CH)

    def rim(i):
        dr, dc = around[i]
        take = [pl.ds(1, 6) if d == 0 else (1 if d < 0 else 6) for d in (dr, dc)]
        put = [pl.ds(1, 6) if d == 0 else (7 if d < 0 else 0) for d in (dr, dc)]
        return pltpu.make_async_remote_copy(
            src_ref=field.at[take[0], take[1]], dst_ref=field.at[put[0], put[1]],
            send_sem=hs.at[i], recv_sem=hr.at[i],
            device_id=at(r + dr, c + dc), device_id_type=MESH,
        )

    for i in range(8):
        rim(i).start()
    wait_all(swap_0 + swap_1 + swap_2 + swap_3)
    for i in range(8):
        rim(i).wait()

    @pl.when(r == 0)
    def _():
        field[0] = jnp.zeros((8, 16, CH), BF16)

    @pl.when(r == 15)
    def _():
        field[7] = jnp.zeros((8, 16, CH), BF16)

    @pl.when(c == 0)
    def _():
        field[:, 0] = jnp.zeros((8, 16, CH), BF16)

    @pl.when(c == 7)
    def _():
        field[:, 7] = jnp.zeros((8, 16, CH), BF16)

    for dy in range(3):
        for dx in range(3):
            win[dy, :, :, :, :, pl.ds(dx * CH, CH)] = field[pl.ds(dy, 6), pl.ds(dx, 6)].reshape(4, 3, 3, 16, CH)

    def to_frame(a, f):
        return pltpu.make_async_remote_copy(
            src_ref=sent.at[a, f], dst_ref=got.at[a, odd * 8 + c],
            send_sem=os_.at[a, f], recv_sem=or_.at[a, odd * 8 + c],
            device_id=(f, lax.div(r, 2)), device_id_type=MESH,
        )

    def stay(a):
        return pltpu.make_async_copy(sent.at[a, r], got.at[a, odd * 8 + c], or_.at[a, odd * 8 + c])

    def self_is(f):
        return jnp.logical_and(own_band, f == r)

    age = lax.broadcasted_iota(jnp.int32, (ROWS, 256), 0) & 15
    for a in range(2):
        def tap(dt, carry):
            total = jnp.zeros((ROWS, 256), F32)
            for dy in range(3):
                rows_w = pl.ds(pl.multiple_of((dt * 3 + dy) * 3 * CH, 16), 3 * CH)
                total += jnp.dot(
                    win[dy].reshape(ROWS, 3 * CH), cw[rows_w, pl.ds(a * 256, 256)], preferred_element_type=F32
                )
            parts[dt] = total
            return carry

        lax.fori_loop(0, 3, tap, 0)
        conv = parts[2]
        conv += jnp.where(age >= 1, pltpu.roll(parts[1], 1, axis=0), 0.0)
        conv += jnp.where(age >= 2, pltpu.roll(parts[0], 2, axis=0), 0.0)
        done = conv.astype(BF16)
        for i in range(6):
            strip = done[96 * i : 96 * i + 96]
            stacked = jnp.concatenate([strip[:, :128], strip[:, 128:]], axis=0)
            moved = jnp.dot(perm[...], stacked, preferred_element_type=F32).astype(BF16)
            sent[a, :, pl.ds(16 * i, 16), :] = moved.reshape(16, 16, 128)

        def ship(f, carry):
            @pl.when(self_is(f))
            def _():
                stay(a).start()

            @pl.when(jnp.logical_not(self_is(f)))
            def _():
                to_frame(a, f).start()

            return carry

        lax.fori_loop(0, 16, ship, 0)

    def arrival(a, i):
        return pltpu.make_async_remote_copy(
            src_ref=sent.at[a, i], dst_ref=got.at[a, i], send_sem=os_.at[a, i], recv_sem=or_.at[a, i],
            device_id=other_core, device_id_type=MESH,
        )

    for a in range(2):
        def collect(i, carry):
            arrival(a, i).wait_recv()
            return carry

        lax.fori_loop(0, 16, collect, 0)
        for half in range(2):
            for i in range(6):
                block = got[a, pl.ds(8 * half, 8), pl.ds(16 * i, 16), :].reshape(128, 128)
                out_ref[12 * half + 2 * i + a] = jnp.dot(
                    back[...], block, preferred_element_type=F32
                ).astype(BF16)

    def drain_group(g, carry):
        @pl.when(g >= GROUPS - 2)
        def _():
            for n in range(3):
                for t in range(3):
                    send(g, n, t).wait_send()

        for t in range(3):
            give(g, t).wait_send()
        return carry

    lax.fori_loop(0, GROUPS, drain_group, 0)
    drain(stage_0 + stage_1 + stage_2 + swap_0 + swap_1 + swap_2 + swap_3)

    def drain_out(f, carry):
        for a in range(2):
            @pl.when(jnp.logical_not(self_is(f)))
            def _():
                to_frame(a, f).wait_send()

        return carry

    lax.fori_loop(0, 16, drain_out, 0)


def local(queries, keys, values, tokens, out_weight, proj_weight, conv_weight):
    cells = [jnp.transpose(a, (1, 2, 0, 3)) for a in (queries, keys, values)]
    rows = jnp.transpose(tokens, (1, 2, 0, 3)).reshape(ROWS, D)
    anywhere = pl.BlockSpec(memory_space=pl.ANY)
    dma = pltpu.SemaphoreType.DMA
    out = pl.pallas_call(
        body,
        out_shape=jax.ShapeDtypeStruct((24, 96, 128), BF16),
        in_specs=[anywhere] * 7,
        out_specs=pl.BlockSpec(memory_space=pltpu.VMEM),
        scratch_shapes=[
            pltpu.VMEM((3, 4, 3, 3, 16, INNER), BF16),
            pltpu.VMEM((4, 3, 3, 16, INNER), BF16),
            pltpu.VMEM((6, 6, 16, INNER), BF16),
            pltpu.VMEM((ROWS, D), F32),
            pltpu.VMEM((ROWS, D), BF16),
            pltpu.VMEM((INNER, D), BF16),
            pltpu.VMEM((D, CH), BF16),
            pltpu.VMEM((16 * SHARD, CH), BF16),
            pltpu.VMEM((SHARD, CH), BF16),
            pltpu.VMEM((8, 8, 16, CH), BF16),
            pltpu.VMEM((ROWS, CH), F32),
            pltpu.VMEM((3, ROWS, 256), F32),
            pltpu.VMEM((256, 192), BF16),
            pltpu.VMEM((96, 128), BF16),
            pltpu.VMEM((2, 16, 96, 128), BF16),
            pltpu.VMEM((2, 16, 96, 128), BF16),
            pltpu.VMEM((ROWS, 1), F32),
            dma((GROUPS, 3, 3)), dma((GROUPS, 3, 3)),
            dma((GROUPS, 3)), dma((GROUPS, 4)),
            dma((7,)),
            dma((48,)), dma((48,)),
            dma((8,)), dma((8,)),
            dma((2, 16)), dma((2, 16)),
        ],
        compiler_params=pltpu.CompilerParams(
            collective_id=0, has_side_effects=True, vmem_limit_bytes=62 * 1024 * 1024
        ),
    )(*cells, rows, out_weight, proj_weight, conv_weight)
    return out[None]


def solution(mesh):
    tile = P(None, "row", "col", None)
    placed = (tile, tile, tile, tile, P(), P(), P("row", None))
    return jax.shard_map(
        local, mesh=mesh, in_specs=placed, out_specs=P("row", "col", None, None), check_vma=False
    )
```

time: 484 us -> 174 us (0.36)
  the two profiles are of different devices: /device:TPU:8 before, /device:TPU:89 now
where the time goes in v1:
time: 174 us
  Pallas kernels  172 us (99%)
  local copies, waits for them, and re-layouts  1.92 us (1%)
    pallas_call x1, Pallas kernels, local(): pl.pallas_call(body, out_shape=jax.ShapeDtypeStruct((24, 96, 128), BF16),...  172 us

profile of v1, /device:TPU:89, one launch (start us, length us, event | category | flops | bytes accessed | tf_op | source)
XLA Modules:
  0.0 173.9 jit_solution(8307814680201398249)
XLA Ops:
  0.0 172.0 %shard_map.73 = bf16[24,96,128]{2,1,0:T(8,128)(2,1)} custom-call(bf16[6,6,16,1536]{3,2,1,0:T(8,128)(2,1)} %bitcast.9, bf16[6,6,16,1536]{3,2,1,0:T(8,128)(2,1)} %bitcast.10, bf16[6,6,16,1536]{3,2,1,0:T(8,128)(2,1)} %bitcast.11, bf16[576,3072]{1,0:T(8,128)(2,1)} %bitcast.7, bf16[1536,3072]{1,0:T(8,128)(2,1)} %wo_ref.1, bf16[3072,512]{1,0:T(8,128)(2,1)} %wp_ref.1, ...), custom_call_target="tpu_custom_call" | custom-call | tf_op jit(solution)/shard_map/pallas_call | solution.py:458
  172.0 1.9 %copy.9 = bf16[1,24,96,128]{3,2,1,0:T(8,128)(2,1)} copy(bf16[1,24,96,128]{3,2,1,0:T(8,128)(2,1)} %bitcast.8) | data formatting | bytes 1179648

commit v2 on v1

v2 whole, which is shorter than its diff:
```python
import math

import jax
import jax.numpy as jnp
from jax import lax
from jax.experimental import pallas as pl
from jax.experimental.pallas import tpu as pltpu
from jax.sharding import PartitionSpec as P

MESH = pl.DeviceIdType.MESH
HEADS = 12
HEAD = 128
GROUPS = 12
WIDE = 128
WINDOW = 2
ORDER = (0, 1, 2)
PAD = 80
INNER = 1536
D = 3072
CH = 512
SHARD = 864
HALF = 432
ROWS = 576
CHUNK = 512
F32 = jnp.float32
BF16 = jnp.bfloat16


def lanes(start, size):
    return pl.ds(pl.multiple_of(start, 128), size)


def body(q_ref, k_ref, v_ref, t_ref, wo_ref, wp_ref, cw_ref, out_ref,
         win, att, home, res, tok, wo, wp, cw, shard, field, acc, perm4, perm2, back, sent, mid, got, ssq,
         fs, fr, rs, rr, ls, ws, wr, hs, hr, os_, or_, cs, cr):
    r = lax.axis_index("row")
    c = lax.axis_index("col")
    odd = lax.rem(r, 2)
    x, zh = lax.div(c, 2), lax.rem(c, 2)
    y, zl = lax.div(r, 4), lax.rem(lax.div(r, 2), 2)

    def at(row, col):
        return (lax.rem(row + 16, 16), lax.rem(col + 8, 8))

    def along_x(step):
        return (r, lax.rem(x + step, 4) * 2 + zh)

    def along_y(step):
        return (lax.rem(y + step, 4) * 4 + zl * 2 + odd, c)

    other_zl = (y * 4 + (1 - zl) * 2 + odd, c)
    other_core = (r + 1 - 2 * odd, c)
    forward = (at(r - 1, c - odd), at(r - 1, c + 1 - odd), at(r, c - 1 + 2 * odd))
    homes = (at(r + 1, c + 1 - odd), at(r + 1, c - odd), at(r, c + 1 - 2 * odd))
    around = [(dr, dc) for dr in (-1, 0, 1) for dc in (-1, 0, 1) if (dr, dc) != (0, 0)]

    barrier = pltpu.get_barrier_semaphore()

    def greet(device):
        pl.semaphore_signal(barrier, inc=1, device_id=device, device_id_type=MESH)

    for step in range(1, 16):
        greet(at(r + step, c))
    for step in range(1, 8):
        greet(at(r, c + step))
    for dr, dc in ((-1, -1), (-1, 1), (1, -1), (1, 1)):
        greet(at(r + dr, c + dc))

    local = [
        pltpu.make_async_copy(cw_ref, shard, ls.at[0]),
        pltpu.make_async_copy(t_ref, tok, ls.at[1]),
        pltpu.make_async_copy(wo_ref, wo, ls.at[2]),
        pltpu.make_async_copy(wp_ref, wp, ls.at[3]),
    ]
    sources = (q_ref, k_ref, v_ref)
    for n in range(3):
        local.append(
            pltpu.make_async_copy(
                sources[n].at[pl.ds(3, 3), pl.ds(3 * (1 - odd), 3)], win.at[n, odd], ls.at[4 + n]
            )
        )
    local[0].start()
    for copy in local[4:]:
        copy.start()

    pl.semaphore_wait(barrier, 26)

    def send(g, n, t):
        span = lanes(g * WIDE, WIDE)
        if t == 2:
            src = sources[n].at[pl.ds(3, 3), pl.ds(3 * odd, 3), :, span]
            dst = win.at[n, 1 - odd, :, :, :, span]
        else:
            src = sources[n].at[pl.ds(0, 3), pl.ds(3 * t, 3), :, span]
            dst = win.at[n, 3 - t, :, :, :, span]
        return pltpu.make_async_remote_copy(
            src_ref=src, dst_ref=dst, send_sem=fs.at[g, n, t], recv_sem=fr.at[g, n, t],
            device_id=forward[t], device_id_type=MESH,
        )

    def give(g, t):
        span = lanes(g * WIDE, WIDE)
        if t == 2:
            src = att.at[1 - odd, :, :, :, span]
            dst = home.at[pl.ds(3, 3), pl.ds(3 * odd, 3), :, span]
        else:
            src = att.at[3 - t, :, :, :, span]
            dst = home.at[pl.ds(0, 3), pl.ds(3 * t, 3), :, span]
        return pltpu.make_async_remote_copy(
            src_ref=src, dst_ref=dst, send_sem=rs.at[g, t], recv_sem=rr.at[g, t],
            device_id=homes[t], device_id_type=MESH,
        )

    def keep(g):
        span = lanes(g * WIDE, WIDE)
        return pltpu.make_async_copy(
            att.at[odd, :, :, :, span], home.at[pl.ds(3, 3), pl.ds(3 * (1 - odd), 3), :, span], rr.at[g, 3]
        )

    def send_group(g):
        for n in range(3):
            for t in ORDER:
                send(g, n, t).start()

    for g in range(WINDOW):
        send_group(g)
    for copy in local[1:4]:
        copy.start()

    quarter = lanes(x * 128, 128)
    everything = pl.ds(0, CH)

    def piece(i, y_, zl_, part, span, device):
        first, size = part
        start = pl.multiple_of((y_ * 4 + zl_ * 2 + odd) * SHARD + first, 16)
        block = cw.at[pl.ds(start, size), span]
        return pltpu.make_async_remote_copy(
            src_ref=block, dst_ref=block, send_sem=ws.at[i], recv_sem=wr.at[i],
            device_id=device, device_id_type=MESH,
        )

    def whose_y(step):
        return lax.rem(y + step, 4)

    low, high, full = (0, HALF), (HALF, HALF), (0, SHARD)
    steps = (1, 3, 2)
    cross = [(0, y, zl, full, quarter, other_zl)]
    own_low = [(s, y, zl, low, quarter, along_y(s)) for s in steps]
    own_high = [(3 + s, y, zl, high, everything, along_y(s)) for s in steps]
    far_low = [(6 + s, y, 1 - zl, low, quarter, along_y(s)) for s in steps]
    far_high = [(9 + s, y, 1 - zl, high, quarter, along_x(s)) for s in steps]
    far_spread = [(12 + s, y, 1 - zl, low, quarter, along_x(s)) for s in steps]
    near = [[(12 + 3 * d + s, whose_y(d), zl, low, quarter, along_x(s)) for s in steps] for d in (1, 2, 3)]
    far_rows = [(24 + s, y, 1 - zl, high, everything, along_y(s)) for s in steps]
    far = [[(24 + 3 * d + s, whose_y(d), 1 - zl, low, quarter, along_x(s)) for s in steps] for d in (1, 2, 3)]
    swap_own = [(37, y, zl, full, everything, other_core)]
    swap_high = [(37 + d, whose_y(d), zl, high, everything, other_core) for d in (1, 2, 3)]
    swap_far = [(41, y, 1 - zl, full, everything, other_core)]
    swap_low = [(41 + d, whose_y(d), zl, low, everything, other_core) for d in (1, 2, 3)]
    swap_rest = [(44 + d, whose_y(d), 1 - zl, full, everything, other_core) for d in (1, 2, 3)]
    swaps = swap_own + swap_high + swap_far + swap_low + swap_rest
    before_groups = cross + own_low + swap_own
    plan = {
        0: ([], own_high[:1]),
        1: (cross, far_low + far_high + own_high[1:2]),
        2: (own_low, far_spread + near[0] + own_high[2:]),
        3: ([], near[1] + near[2]),
        4: (far_high, far_rows[:1]),
        5: (far_low, far_rows[1:2] + far[0]),
        6: ([], far_rows[2:] + far[1]),
        7: (own_high, far[2] + swap_high),
        8: (far_spread, swap_far),
        9: (near[0] + near[1] + near[2], swap_low),
        10: (far_rows + far[0] + far[1] + far[2], swap_rest),
    }
    pieces_sent = before_groups + [item for _, leaving in plan.values() for item in leaving]

    def start_all(pieces):
        for item in pieces:
            piece(*item).start()

    def wait_all(pieces):
        for item in pieces:
            piece(*item).wait_recv()

    def drain(pieces):
        for item in pieces:
            piece(*item).wait_send()

    local[0].wait()
    key = lax.broadcasted_iota(jnp.int32, (CH, CH), 0)
    lane = lax.broadcasted_iota(jnp.int32, (CH, CH), 1)
    order = jnp.where(key == 4 * (lane & 127) + (lane >> 7), 1.0, 0.0).astype(BF16)
    own_start = pl.multiple_of(r * SHARD, 16)
    for part in range(3):
        cw[pl.ds(own_start + 288 * part, 288), :] = jnp.dot(
            shard[pl.ds(288 * part, 288), :], order, preferred_element_type=F32
        ).astype(BF16)
    start_all(before_groups)

    def reorder(count, size):
        shape = (16 * size, count * 192)
        row = lax.broadcasted_iota(jnp.int32, shape, 0)
        col = lax.broadcasted_iota(jnp.int32, shape, 1)
        frame = row >> 4
        if size == 48:
            frame = (row * 21846) >> 20
        elif size == 32:
            frame = row >> 5
        place = row - frame * size
        strip = (place * 171) >> 11
        across = place - strip * 12
        wanted = (across & 1) * (count * 96) + strip * 96 + (across >> 1) * 16 + frame
        return jnp.where(jnp.logical_and(place < 12 * count, col == wanted), 1.0, 0.0).astype(BF16)

    perm4[...] = reorder(4, 48)
    perm2[...] = reorder(2, 32)
    row = lax.broadcasted_iota(jnp.int32, (ROWS, 8 * PAD), 0)
    col = lax.broadcasted_iota(jnp.int32, (ROWS, 8 * PAD), 1)
    strip = (row * 683) >> 16
    place = row - strip * 96
    which = (place * 171) >> 11
    wanted = which * PAD + strip * 12 + place - which * 12
    back[...] = jnp.where(col == wanted, 1.0, 0.0).astype(BF16)

    for copy in local[4:]:
        copy.wait()

    def attend(h):
        span = lanes(h * HEAD, HEAD)
        keys = win[1, :, :, :, :, span].reshape(ROWS, HEAD)
        values = win[2, :, :, :, :, span].reshape(ROWS, HEAD)
        for part in range(2):
            queries = win[0, pl.ds(2 * part, 2), :, :, :, span].reshape(ROWS // 2, HEAD)
            scores = lax.dot_general(
                queries, keys, (((1,), (1,)), ((), ())), preferred_element_type=F32
            ) * (1.0 / math.sqrt(HEAD))
            highest = jnp.max(scores, axis=-1, keepdims=True)
            weights = jnp.exp(scores - highest)
            probs = (weights * (1.0 / jnp.sum(weights, axis=-1, keepdims=True))).astype(BF16)
            mixed = jnp.dot(probs, values, preferred_element_type=F32).astype(BF16)
            att[pl.ds(2 * part, 2), :, :, :, span] = mixed.reshape(2, 3, 3, 16, HEAD)

    def await_home(g):
        for t in range(3):
            give(g, t).wait_recv()
        keep(g).wait()

    def add_pair(g, first):
        await_home(g)
        await_home(g + 1)
        rows = home[:, :, :, lanes(g * WIDE, 2 * WIDE)].reshape(ROWS, 2 * WIDE)

        def chunk(n, carry):
            span = lanes(n * CHUNK, CHUNK)
            product = jnp.dot(
                rows, wo[pl.ds(pl.multiple_of(g * WIDE, WIDE), 2 * WIDE), span], preferred_element_type=F32
            )
            base = tok[:, span].astype(F32) if first else res[:, span]
            res[:, span] = base + product
            return carry

        lax.fori_loop(0, D // CHUNK, chunk, 0)

    def group(g, carry):
        for n in range(3):
            for t in range(3):
                send(g, n, t).wait_recv()

        @pl.when(g < GROUPS - WINDOW)
        def _():
            for n in range(3):
                for t in range(3):
                    send(g, n, t).wait_send()
            send_group(g + WINDOW)

        for h in range(WIDE // HEAD):
            attend(g * (WIDE // HEAD) + h)
        for t in ORDER:
            give(g, t).start()
        keep(g).start()

        def weights_step(arriving, leaving):
            def _():
                wait_all(arriving)
                start_all(leaving)

            return _

        for at_group, (arriving, leaving) in plan.items():
            pl.when(g == at_group)(weights_step(arriving, leaving))

        @pl.when(g == 2)
        def _():
            for copy in local[1:4]:
                copy.wait()
            add_pair(0, True)

        @pl.when(jnp.logical_and(g > 2, lax.rem(g, 2) == 0))
        def _():
            add_pair(g - 2, False)

        return carry

    lax.fori_loop(0, GROUPS, group, 0)

    last = GROUPS - 2
    await_home(last)
    await_home(last + 1)
    rows = home[:, :, :, pl.ds(last * WIDE, 2 * WIDE)].reshape(ROWS, 2 * WIDE)
    ssq[...] = jnp.zeros_like(ssq)
    acc[...] = jnp.zeros_like(acc)

    def finish(n, carry):
        span = lanes(n * CHUNK, CHUNK)
        total = res[:, span] + jnp.dot(rows, wo[pl.ds(last * WIDE, 2 * WIDE), span], preferred_element_type=F32)
        ssq[...] += jnp.sum(total * total, axis=-1, keepdims=True)
        acc[...] += jnp.dot(
            total.astype(BF16), wp[pl.ds(pl.multiple_of(n * CHUNK, CHUNK), CHUNK), :], preferred_element_type=F32
        )
        return carry

    lax.fori_loop(0, D // CHUNK, finish, 0)
    raw = acc[...] * lax.rsqrt(ssq[...] * (1.0 / D) + 1e-6)
    features = (raw / (1.0 + jnp.exp(-raw))).astype(BF16)
    field[pl.ds(1, 6), pl.ds(1, 6)] = features.reshape(6, 6, 16, CH)

    def rim(i):
        dr, dc = around[i]
        take = [pl.ds(1, 6) if d == 0 else (1 if d < 0 else 6) for d in (dr, dc)]
        put = [pl.ds(1, 6) if d == 0 else (7 if d < 0 else 0) for d in (dr, dc)]
        return pltpu.make_async_remote_copy(
            src_ref=field.at[take[0], take[1]], dst_ref=field.at[put[0], put[1]],
            send_sem=hs.at[i], recv_sem=hr.at[i],
            device_id=at(r + dr, c + dc), device_id_type=MESH,
        )

    sides = (0, 2, 3, 4, 5, 7)
    for i in sides + (1, 6):
        rim(i).start()
    wait_all(swaps)
    for i in (1, 6):
        rim(i).wait()

    @pl.when(r == 0)
    def _():
        field[0, pl.ds(1, 6)] = jnp.zeros((6, 16, CH), BF16)

    @pl.when(r == 15)
    def _():
        field[7, pl.ds(1, 6)] = jnp.zeros((6, 16, CH), BF16)

    def tap_rows(dt, dy, dx):
        return pl.ds(pl.multiple_of(((dt * 3 + dy) * 3 + dx) * CH, CH), CH)

    def centre(step, carry):
        a, dt = lax.div(step, 3), lax.rem(step, 3)
        total = jnp.zeros((ROWS, 256), F32)
        for dy in range(3):
            total += jnp.dot(
                field[pl.ds(dy, 6), pl.ds(1, 6)].reshape(ROWS, CH), cw[tap_rows(dt, dy, 1), lanes(a * 256, 256)],
                preferred_element_type=F32,
            )
        res[:, lanes(step * 256, 256)] = total
        return carry

    lax.fori_loop(0, 6, centre, 0)

    for i in sides:
        rim(i).wait()

    @pl.when(r == 0)
    def _():
        field[0] = jnp.zeros((8, 16, CH), BF16)

    @pl.when(r == 15)
    def _():
        field[7] = jnp.zeros((8, 16, CH), BF16)

    @pl.when(c == 0)
    def _():
        field[:, 0] = jnp.zeros((8, 16, CH), BF16)

    @pl.when(c == 7)
    def _():
        field[:, 7] = jnp.zeros((8, 16, CH), BF16)

    def to_row(a, f):
        return pltpu.make_async_remote_copy(
            src_ref=sent.at[a, f], dst_ref=mid.at[a, r], send_sem=os_.at[a, f], recv_sem=or_.at[a, r],
            device_id=(f, c), device_id_type=MESH,
        )

    def row_arrival(a, i):
        return pltpu.make_async_remote_copy(
            src_ref=sent.at[a, i], dst_ref=mid.at[a, i], send_sem=os_.at[a, i], recv_sem=or_.at[a, i],
            device_id=(i, c), device_id_type=MESH,
        )

    def row_stay(a):
        return pltpu.make_async_copy(sent.at[a, r], mid.at[a, r], or_.at[a, r])

    def to_col(a, col):
        return pltpu.make_async_remote_copy(
            src_ref=mid.at[a, pl.ds(2 * col, 2)], dst_ref=got.at[a, :, c], send_sem=cs.at[a, col], recv_sem=cr.at[a, c],
            device_id=(r, col), device_id_type=MESH,
        )

    def col_arrival(a, i):
        return pltpu.make_async_remote_copy(
            src_ref=mid.at[a, pl.ds(0, 2)], dst_ref=got.at[a, :, i], send_sem=cs.at[a, i], recv_sem=cr.at[a, i],
            device_id=(r, i), device_id_type=MESH,
        )

    def col_stay(a):
        return pltpu.make_async_copy(mid.at[a, pl.ds(2 * c, 2)], got.at[a, :, c], cr.at[a, c])

    age = lax.broadcasted_iota(jnp.int32, (ROWS, 256), 0) & 15

    def convolve(a):
        def tap(dt, carry):
            spot = lanes((a * 3 + dt) * 256, 256)
            total = res[:, spot]
            for dy in range(3):
                for dx in (0, 2):
                    total += jnp.dot(
                        field[pl.ds(dy, 6), pl.ds(dx, 6)].reshape(ROWS, CH),
                        cw[tap_rows(dt, dy, dx), pl.ds(a * 256, 256)],
                        preferred_element_type=F32,
                    )
            res[:, spot] = total
            return carry

        lax.fori_loop(0, 3, tap, 0)
        first = a * 768
        conv = res[:, first + 512 : first + 768]
        conv += jnp.where(age >= 1, pltpu.roll(res[:, first + 256 : first + 512], 1, axis=0), 0.0)
        conv += jnp.where(age >= 2, pltpu.roll(res[:, first : first + 256], 2, axis=0), 0.0)
        done = conv.astype(BF16)
        for rows, table, start, size in ((done[:384], perm4, 0, 48), (done[384:], perm2, 48, 32)):
            stacked = jnp.concatenate([rows[:, :128], rows[:, 128:]], axis=0)
            moved = jnp.dot(table[...], stacked, preferred_element_type=F32).astype(BF16)
            sent[a, :, pl.ds(start, size), :] = moved.reshape(16, size, 128)

        row_stay(a).start()
        for step in range(1, 16):
            to_row(a, lax.rem(r + step, 16)).start()

    def pass_on(a):
        row_stay(a).wait()
        for step in range(1, 16):
            row_arrival(a, lax.rem(r + step, 16)).wait_recv()
        col_stay(a).start()
        for step in range(1, 8):
            to_col(a, lax.rem(c + step, 8)).start()

    def collect(a):
        col_stay(a).wait()
        for step in range(1, 8):
            col_arrival(a, lax.rem(c + step, 8)).wait_recv()
        for half in range(2):
            block = jnp.dot(
                back[...], got[a, half].reshape(8 * PAD, 128), preferred_element_type=F32
            ).astype(BF16)
            for i in range(6):
                out_ref[12 * half + 2 * i + a] = block[96 * i : 96 * i + 96]

    convolve(0)
    convolve(1)
    pass_on(0)
    pass_on(1)
    collect(0)
    collect(1)

    def drain_group(g, carry):
        @pl.when(g >= GROUPS - WINDOW)
        def _():
            for n in range(3):
                for t in range(3):
                    send(g, n, t).wait_send()

        for t in range(3):
            give(g, t).wait_send()
        return carry

    lax.fori_loop(0, GROUPS, drain_group, 0)
    drain(pieces_sent)

    for a in range(2):
        for step in range(1, 16):
            to_row(a, lax.rem(r + step, 16)).wait_send()
        for step in range(1, 8):
            to_col(a, lax.rem(c + step, 8)).wait_send()


def local(queries, keys, values, tokens, out_weight, proj_weight, conv_weight):
    cells = [jnp.transpose(a, (1, 2, 0, 3)) for a in (queries, keys, values)]
    rows = jnp.transpose(tokens, (1, 2, 0, 3)).reshape(ROWS, D)
    anywhere = pl.BlockSpec(memory_space=pl.ANY)
    dma = pltpu.SemaphoreType.DMA
    out = pl.pallas_call(
        body,
        out_shape=jax.ShapeDtypeStruct((24, 96, 128), BF16),
        in_specs=[anywhere] * 7,
        out_specs=pl.BlockSpec(memory_space=pltpu.VMEM),
        scratch_shapes=[
            pltpu.VMEM((3, 4, 3, 3, 16, INNER), BF16),
            pltpu.VMEM((4, 3, 3, 16, INNER), BF16),
            pltpu.VMEM((6, 6, 16, INNER), BF16),
            pltpu.VMEM((ROWS, D), F32),
            pltpu.VMEM((ROWS, D), BF16),
            pltpu.VMEM((INNER, D), BF16),
            pltpu.VMEM((D, CH), BF16),
            pltpu.VMEM((16 * SHARD, CH), BF16),
            pltpu.VMEM((SHARD, CH), BF16),
            pltpu.VMEM((8, 8, 16, CH), BF16),
            pltpu.VMEM((ROWS, CH), F32),
            pltpu.VMEM((768, 768), BF16),
            pltpu.VMEM((512, 384), BF16),
            pltpu.VMEM((ROWS, 8 * PAD), BF16),
            pltpu.VMEM((2, 16, PAD, 128), BF16),
            pltpu.VMEM((2, 16, PAD, 128), BF16),
            pltpu.VMEM((2, 2, 8, PAD, 128), BF16),
            pltpu.VMEM((ROWS, 1), F32),
            dma((GROUPS, 3, 3)), dma((GROUPS, 3, 3)),
            dma((GROUPS, 3)), dma((GROUPS, 4)),
            dma((7,)),
            dma((48,)), dma((48,)),
            dma((8,)), dma((8,)),
            dma((2, 16)), dma((2, 16)),
            dma((2, 8)), dma((2, 8)),
        ],
        compiler_params=pltpu.CompilerParams(
            collective_id=0, has_side_effects=True, vmem_limit_bytes=62 * 1024 * 1024
        ),
    )(*cells, rows, out_weight, proj_weight, conv_weight)
    return out[None]


def solution(mesh):
    tile = P(None, "row", "col", None)
    placed = (tile, tile, tile, tile, P(), P(), P("row", None))
    return jax.shard_map(
        local, mesh=mesh, in_specs=placed, out_specs=P("row", "col", None, None), check_vma=False
    )
```

time: 174 us -> 156 us (0.90)
  the two profiles are of different devices: /device:TPU:89 before, /device:TPU:8 now
where the time goes in v2:
time: 156 us; the launch traced here: 154 us
  Pallas kernels  152 us (97%)
  local copies, waits for them, and re-layouts  1.92 us (1%)
    pallas_call x1, Pallas kernels, local(): pl.pallas_call(body, out_shape=jax.ShapeDtypeStruct((24, 96, 128), BF16),...  152 us

profile of v2, /device:TPU:8, one launch (start us, length us, event | category | flops | bytes accessed | tf_op | source)
XLA Modules:
  0.0 153.5 jit_solution(7173194472229203482)
XLA Ops:
  0.0 151.6 %shard_map.73 = bf16[24,96,128]{2,1,0:T(8,128)(2,1)} custom-call(bf16[6,6,16,1536]{3,2,1,0:T(8,128)(2,1)} %bitcast.9, bf16[6,6,16,1536]{3,2,1,0:T(8,128)(2,1)} %bitcast.10, bf16[6,6,16,1536]{3,2,1,0:T(8,128)(2,1)} %bitcast.11, bf16[576,3072]{1,0:T(8,128)(2,1)} %bitcast.7, bf16[1536,3072]{1,0:T(8,128)(2,1)} %wo_ref.1, bf16[3072,512]{1,0:T(8,128)(2,1)} %wp_ref.1, ...), custom_call_target="tpu_custom_call" | custom-call | tf_op jit(solution)/shard_map/pallas_call | solution.py:501
  151.6 1.9 %copy.9 = bf16[1,24,96,128]{3,2,1,0:T(8,128)(2,1)} copy(bf16[1,24,96,128]{3,2,1,0:T(8,128)(2,1)} %bitcast.8) | data formatting | bytes 1179648

commit v3 on v2

--- a/solution.py
+++ b/solution.py
@@ -31,7 +31,7 @@
 
 
 def body(q_ref, k_ref, v_ref, t_ref, wo_ref, wp_ref, cw_ref, out_ref,
-         win, att, home, res, tok, wo, wp, cw, shard, field, acc, perm4, perm2, back, sent, mid, got, ssq,
+         win, att, home, res, tok, wo, wp, cw, shard, field, acc, perm4, perm2, back, sent, mid, got, both,
          fs, fr, rs, rr, ls, ws, wr, hs, hr, os_, or_, cs, cr):
     r = lax.axis_index("row")
     c = lax.axis_index("col")
@@ -59,12 +59,21 @@
     def greet(device):
         pl.semaphore_signal(barrier, inc=1, device_id=device, device_id_type=MESH)
 
-    for step in range(1, 16):
-        greet(at(r + step, c))
-    for step in range(1, 8):
-        greet(at(r, c + step))
-    for dr, dc in ((-1, -1), (-1, 1), (1, -1), (1, 1)):
+    for dr, dc in around:
         greet(at(r + dr, c + dc))
+    for step in (1, 2, 3):
+        greet(along_x(step))
+        greet(along_y(step))
+    greet(other_zl)
+    greet(other_core)
+    own_corner = zl == zh
+    for half in range(2):
+        for col in range(8):
+            row = 4 * y + 2 * zh + half
+
+            @pl.when(jnp.logical_or(row != r, col != c))
+            def _(row=row, col=col):
+                greet((row, col))
 
     local = [
         pltpu.make_async_copy(cw_ref, shard, ls.at[0]),
@@ -83,7 +92,7 @@
     for copy in local[4:]:
         copy.start()
 
-    pl.semaphore_wait(barrier, 26)
+    pl.semaphore_wait(barrier, 32 - own_corner.astype(jnp.int32))
 
     def send(g, n, t):
         span = lanes(g * WIDE, WIDE)
@@ -256,17 +265,31 @@
             product = jnp.dot(
                 rows, wo[pl.ds(pl.multiple_of(g * WIDE, WIDE), 2 * WIDE), span], preferred_element_type=F32
             )
-            base = tok[:, span].astype(F32) if first else res[:, span]
-            res[:, span] = base + product
+            base = tok[:, span].astype(F32) if first else res[:, :, :, span].reshape(ROWS, CHUNK)
+            res[:, :, :, span] = (base + product).reshape(6, 6, 16, CHUNK)
             return carry
 
         lax.fori_loop(0, D // CHUNK, chunk, 0)
 
+    last = GROUPS - 2
+
+    def merge():
+        both[...] = jnp.dot(
+            wo[pl.ds(last * WIDE, 2 * WIDE), :], wp[...], preferred_element_type=F32
+        ).astype(BF16)
+
+    def project():
+        acc[...] = jnp.zeros_like(acc)
+
+        def chunk(n, carry):
+            rows = pl.ds(pl.multiple_of(n * CHUNK, CHUNK), CHUNK)
+            known = res[:, :, :, lanes(n * CHUNK, CHUNK)].reshape(ROWS, CHUNK).astype(BF16)
+            acc[...] += jnp.dot(known, wp[rows, :], preferred_element_type=F32).reshape(6, 6, 16, CH)
+            return carry
+
+        lax.fori_loop(0, D // CHUNK, chunk, 0)
+
     def group(g, carry):
-        for n in range(3):
-            for t in range(3):
-                send(g, n, t).wait_recv()
-
         @pl.when(g < GROUPS - WINDOW)
         def _():
             for n in range(3):
@@ -274,6 +297,28 @@
                     send(g, n, t).wait_send()
             send_group(g + WINDOW)
 
+        @pl.when(g == 3)
+        def _():
+            for copy in local[1:4]:
+                copy.wait()
+            add_pair(0, True)
+
+        @pl.when(jnp.logical_and(g > 3, lax.rem(g, 2) == 1))
+        def _():
+            add_pair(g - 3, False)
+
+        @pl.when(g == GROUPS - 2)
+        def _():
+            merge()
+
+        @pl.when(g == GROUPS - 1)
+        def _():
+            project()
+
+        for n in range(3):
+            for t in range(3):
+                send(g, n, t).wait_recv()
+
         for h in range(WIDE // HEAD):
             attend(g * (WIDE // HEAD) + h)
         for t in ORDER:
@@ -290,41 +335,12 @@
         for at_group, (arriving, leaving) in plan.items():
             pl.when(g == at_group)(weights_step(arriving, leaving))
 
-        @pl.when(g == 2)
-        def _():
-            for copy in local[1:4]:
-                copy.wait()
-            add_pair(0, True)
-
-        @pl.when(jnp.logical_and(g > 2, lax.rem(g, 2) == 0))
-        def _():
-            add_pair(g - 2, False)
-
         return carry
 
     lax.fori_loop(0, GROUPS, group, 0)
 
-    last = GROUPS - 2
     await_home(last)
     await_home(last + 1)
-    rows = home[:, :, :, pl.ds(last * WIDE, 2 * WIDE)].reshape(ROWS, 2 * WIDE)
-    ssq[...] = jnp.zeros_like(ssq)
-    acc[...] = jnp.zeros_like(acc)
-
-    def finish(n, carry):
-        span = lanes(n * CHUNK, CHUNK)
-        total = res[:, span] + jnp.dot(rows, wo[pl.ds(last * WIDE, 2 * WIDE), span], preferred_element_type=F32)
-        ssq[...] += jnp.sum(total * total, axis=-1, keepdims=True)
-        acc[...] += jnp.dot(
-            total.astype(BF16), wp[pl.ds(pl.multiple_of(n * CHUNK, CHUNK), CHUNK), :], preferred_element_type=F32
-        )
-        return carry
-
-    lax.fori_loop(0, D // CHUNK, finish, 0)
-    raw = acc[...] * lax.rsqrt(ssq[...] * (1.0 / D) + 1e-6)
-    features = (raw / (1.0 + jnp.exp(-raw))).astype(BF16)
-    field[pl.ds(1, 6), pl.ds(1, 6)] = features.reshape(6, 6, 16, CH)
-
     def rim(i):
         dr, dc = around[i]
         take = [pl.ds(1, 6) if d == 0 else (1 if d < 0 else 6) for d in (dr, dc)]
@@ -335,8 +351,37 @@
             device_id=at(r + dr, c + dc), device_id_type=MESH,
         )
 
+    def columns(ref, spans, span):
+        blocks = [ref[:, pl.ds(j, n), :, span] for j, n in spans]
+        blocks = [block.reshape(-1, block.shape[-1]) for block in blocks]
+        return blocks[0] if len(blocks) == 1 else jnp.concatenate(blocks, axis=0)
+
+    def finish(spans):
+        count = 96 * sum(n for _, n in spans)
+        rows = columns(home, spans, pl.ds(last * WIDE, 2 * WIDE))
+
+        def chunk(n, squares):
+            span = lanes(n * CHUNK, CHUNK)
+            total = columns(res, spans, span) + jnp.dot(
+                rows, wo[pl.ds(last * WIDE, 2 * WIDE), span], preferred_element_type=F32
+            )
+            return squares + jnp.sum(total * total, axis=-1, keepdims=True)
+
+        squares = lax.fori_loop(0, D // CHUNK, chunk, jnp.zeros((count, 1), F32))
+        raw = columns(acc, spans, pl.ds(0, CH)) + jnp.dot(rows, both[...], preferred_element_type=F32)
+        raw = raw * lax.rsqrt(squares * (1.0 / D) + 1e-6)
+        features = (raw / (1.0 + jnp.exp(-raw))).astype(BF16)
+        start = 0
+        for j, n in spans:
+            field[pl.ds(1, 6), pl.ds(1 + j, n)] = features[start : start + 96 * n].reshape(6, n, 16, CH)
+            start += 96 * n
+
     sides = (0, 2, 3, 4, 5, 7)
-    for i in sides + (1, 6):
+    finish(((0, 1), (5, 1)))
+    for i in sides:
+        rim(i).start()
+    finish(((1, 4),))
+    for i in (1, 6):
         rim(i).start()
     wait_all(swaps)
     for i in (1, 6):
@@ -353,18 +398,18 @@
     def tap_rows(dt, dy, dx):
         return pl.ds(pl.multiple_of(((dt * 3 + dy) * 3 + dx) * CH, CH), CH)
 
-    def centre(step, carry):
-        a, dt = lax.div(step, 3), lax.rem(step, 3)
-        total = jnp.zeros((ROWS, 256), F32)
+    def centre(dt, carry):
+        total = jnp.zeros((ROWS, CH), F32)
         for dy in range(3):
             total += jnp.dot(
-                field[pl.ds(dy, 6), pl.ds(1, 6)].reshape(ROWS, CH), cw[tap_rows(dt, dy, 1), lanes(a * 256, 256)],
+                field[pl.ds(dy, 6), pl.ds(1, 6)].reshape(ROWS, CH), cw[tap_rows(dt, dy, 1), :],
                 preferred_element_type=F32,
             )
-        res[:, lanes(step * 256, 256)] = total
+        res[:, :, :, lanes(dt * 256, 256)] = total[:, :256].reshape(6, 6, 16, 256)
+        res[:, :, :, lanes((dt + 3) * 256, 256)] = total[:, 256:].reshape(6, 6, 16, 256)
         return carry
 
-    lax.fori_loop(0, 6, centre, 0)
+    lax.fori_loop(0, 3, centre, 0)
 
     for i in sides:
         rim(i).wait()
@@ -385,42 +430,54 @@
     def _():
         field[:, 7] = jnp.zeros((8, 16, CH), BF16)
 
-    def to_row(a, f):
+    def to_y(a, step):
+        there = whose_y(step)
         return pltpu.make_async_remote_copy(
-            src_ref=sent.at[a, f], dst_ref=mid.at[a, r], send_sem=os_.at[a, f], recv_sem=or_.at[a, r],
-            device_id=(f, c), device_id_type=MESH,
-        )
-
-    def row_arrival(a, i):
+            src_ref=sent.at[a, pl.ds(4 * there, 4)], dst_ref=mid.at[a, y],
+            send_sem=os_.at[a, step], recv_sem=or_.at[a, step], device_id=along_y(step), device_id_type=MESH,
+        )
+
+    def hop(a, step, e):
+        origin = whose_y(step)
+        block = sent.at[a, 4 * y + e] if step == 0 else mid.at[a, origin, e]
+        return origin, block
+
+    def mine(origin, e):
+        return jnp.logical_and(own_corner, jnp.logical_and(origin == x, e == 2 * zl + odd))
+
+    def to_owner(a, step, e):
+        origin, block = hop(a, step, e)
         return pltpu.make_async_remote_copy(
-            src_ref=sent.at[a, i], dst_ref=mid.at[a, i], send_sem=os_.at[a, i], recv_sem=or_.at[a, i],
-            device_id=(i, c), device_id_type=MESH,
-        )
-
-    def row_stay(a):
-        return pltpu.make_async_copy(sent.at[a, r], mid.at[a, r], or_.at[a, r])
-
-    def to_col(a, col):
+            src_ref=block, dst_ref=got.at[a, odd, c], send_sem=cs.at[a, 4 * step + e], recv_sem=cr.at[a, odd, c],
+            device_id=(4 * y + e, 2 * origin + zl), device_id_type=MESH,
+        )
+
+    def own(a, step, e):
+        _, block = hop(a, step, e)
+        return pltpu.make_async_copy(block, got.at[a, odd, c], cr.at[a, odd, c])
+
+    def arrival(a, half, col):
         return pltpu.make_async_remote_copy(
-            src_ref=mid.at[a, pl.ds(2 * col, 2)], dst_ref=got.at[a, :, c], send_sem=cs.at[a, col], recv_sem=cr.at[a, c],
-            device_id=(r, col), device_id_type=MESH,
-        )
-
-    def col_arrival(a, i):
-        return pltpu.make_async_remote_copy(
-            src_ref=mid.at[a, pl.ds(0, 2)], dst_ref=got.at[a, :, i], send_sem=cs.at[a, i], recv_sem=cr.at[a, i],
-            device_id=(r, i), device_id_type=MESH,
-        )
-
-    def col_stay(a):
-        return pltpu.make_async_copy(mid.at[a, pl.ds(2 * c, 2)], got.at[a, :, c], cr.at[a, c])
+            src_ref=sent.at[a, 0], dst_ref=got.at[a, half, col], send_sem=cs.at[a, 0], recv_sem=cr.at[a, half, col],
+            device_id=other_core, device_id_type=MESH,
+        )
+
+    def spread(a, step):
+        for e in range(4):
+            @pl.when(mine(whose_y(step), e))
+            def _(e=e):
+                own(a, step, e).start()
+
+            @pl.when(jnp.logical_not(mine(whose_y(step), e)))
+            def _(e=e):
+                to_owner(a, step, e).start()
 
     age = lax.broadcasted_iota(jnp.int32, (ROWS, 256), 0) & 15
 
     def convolve(a):
         def tap(dt, carry):
             spot = lanes((a * 3 + dt) * 256, 256)
-            total = res[:, spot]
+            total = res[:, :, :, spot].reshape(ROWS, 256)
             for dy in range(3):
                 for dx in (0, 2):
                     total += jnp.dot(
@@ -428,36 +485,33 @@
                         cw[tap_rows(dt, dy, dx), pl.ds(a * 256, 256)],
                         preferred_element_type=F32,
                     )
-            res[:, spot] = total
+            res[:, :, :, spot] = total.reshape(6, 6, 16, 256)
             return carry
 
         lax.fori_loop(0, 3, tap, 0)
-        first = a * 768
-        conv = res[:, first + 512 : first + 768]
-        conv += jnp.where(age >= 1, pltpu.roll(res[:, first + 256 : first + 512], 1, axis=0), 0.0)
-        conv += jnp.where(age >= 2, pltpu.roll(res[:, first : first + 256], 2, axis=0), 0.0)
+        taps = [res[:, :, :, pl.ds((a * 3 + dt) * 256, 256)].reshape(ROWS, 256) for dt in range(3)]
+        conv = taps[2]
+        conv += jnp.where(age >= 1, pltpu.roll(taps[1], 1, axis=0), 0.0)
+        conv += jnp.where(age >= 2, pltpu.roll(taps[0], 2, axis=0), 0.0)
         done = conv.astype(BF16)
         for rows, table, start, size in ((done[:384], perm4, 0, 48), (done[384:], perm2, 48, 32)):
             stacked = jnp.concatenate([rows[:, :128], rows[:, 128:]], axis=0)
             moved = jnp.dot(table[...], stacked, preferred_element_type=F32).astype(BF16)
             sent[a, :, pl.ds(start, size), :] = moved.reshape(16, size, 128)
 
-        row_stay(a).start()
-        for step in range(1, 16):
-            to_row(a, lax.rem(r + step, 16)).start()
+        for step in (2, 1, 3):
+            to_y(a, step).start()
+        spread(a, 0)
 
     def pass_on(a):
-        row_stay(a).wait()
-        for step in range(1, 16):
-            row_arrival(a, lax.rem(r + step, 16)).wait_recv()
-        col_stay(a).start()
-        for step in range(1, 8):
-            to_col(a, lax.rem(c + step, 8)).start()
+        for step in (1, 3, 2):
+            to_y(a, 4 - step).wait_recv()
+            spread(a, step)
 
     def collect(a):
-        col_stay(a).wait()
-        for step in range(1, 8):
-            col_arrival(a, lax.rem(c + step, 8)).wait_recv()
+        for half in range(2):
+            for col in range(8):
+                arrival(a, half, col).wait_recv()
         for half in range(2):
             block = jnp.dot(
                 back[...], got[a, half].reshape(8 * PAD, 128), preferred_element_type=F32
@@ -487,10 +541,13 @@
     drain(pieces_sent)
 
     for a in range(2):
-        for step in range(1, 16):
-            to_row(a, lax.rem(r + step, 16)).wait_send()
-        for step in range(1, 8):
-            to_col(a, lax.rem(c + step, 8)).wait_send()
+        for step in range(4):
+            if step:
+                to_y(a, step).wait_send()
+            for e in range(4):
+                @pl.when(jnp.logical_not(mine(whose_y(step), e)))
+                def _(a=a, step=step, e=e):
+                    to_owner(a, step, e).wait_send()
 
 
 def local(queries, keys, values, tokens, out_weight, proj_weight, conv_weight):
@@ -507,28 +564,28 @@
             pltpu.VMEM((3, 4, 3, 3, 16, INNER), BF16),
             pltpu.VMEM((4, 3, 3, 16, INNER), BF16),
             pltpu.VMEM((6, 6, 16, INNER), BF16),
-            pltpu.VMEM((ROWS, D), F32),
+            pltpu.VMEM((6, 6, 16, D), F32),
             pltpu.VMEM((ROWS, D), BF16),
             pltpu.VMEM((INNER, D), BF16),
             pltpu.VMEM((D, CH), BF16),
             pltpu.VMEM((16 * SHARD, CH), BF16),
             pltpu.VMEM((SHARD, CH), BF16),
             pltpu.VMEM((8, 8, 16, CH), BF16),
-            pltpu.VMEM((ROWS, CH), F32),
+            pltpu.VMEM((6, 6, 16, CH), F32),
             pltpu.VMEM((768, 768), BF16),
             pltpu.VMEM((512, 384), BF16),
             pltpu.VMEM((ROWS, 8 * PAD), BF16),
             pltpu.VMEM((2, 16, PAD, 128), BF16),
-            pltpu.VMEM((2, 16, PAD, 128), BF16),
+            pltpu.VMEM((2, 4, 4, PAD, 128), BF16),
             pltpu.VMEM((2, 2, 8, PAD, 128), BF16),
-            pltpu.VMEM((ROWS, 1), F32),
+            pltpu.VMEM((2 * WIDE, CH), BF16),
             dma((GROUPS, 3, 3)), dma((GROUPS, 3, 3)),
             dma((GROUPS, 3)), dma((GROUPS, 4)),
             dma((7,)),
             dma((48,)), dma((48,)),
             dma((8,)), dma((8,)),
-            dma((2, 16)), dma((2, 16)),
-            dma((2, 8)), dma((2, 8)),
+            dma((2, 4)), dma((2, 4)),
+            dma((2, 16)), dma((2, 2, 8)),
         ],
         compiler_params=pltpu.CompilerParams(
             collective_id=0, has_side_effects=True, vmem_limit_bytes=62 * 1024 * 1024

time: 156 us -> 151 us (0.968); the launches traced: 154 us -> 150 us
  Pallas kernels: 152 us -> 148 us
    pallas_call x1, Pallas kernels: 152 us -> 148 us  [local(): pl.pallas_call(body, out_shape=jax.ShapeDtypeStruct((24, 96, 128), BF16),...]
where the time goes in v3:
time: 151 us; the launch traced here: 150 us
  Pallas kernels  148 us (98%)
  local copies, waits for them, and re-layouts  1.92 us (1%)
    pallas_call x1, Pallas kernels, local(): pl.pallas_call(body, out_shape=jax.ShapeDtypeStruct((24, 96, 128), BF16),...  148 us

profile of v3, /device:TPU:8, one launch (start us, length us, event | category | flops | bytes accessed | tf_op | source)
XLA Modules:
  0.0 150.2 jit_solution(10085874380672085291)
XLA Ops:
  0.0 148.3 %shard_map.73 = bf16[24,96,128]{2,1,0:T(8,128)(2,1)} custom-call(bf16[6,6,16,1536]{3,2,1,0:T(8,128)(2,1)} %bitcast.9, bf16[6,6,16,1536]{3,2,1,0:T(8,128)(2,1)} %bitcast.10, bf16[6,6,16,1536]{3,2,1,0:T(8,128)(2,1)} %bitcast.11, bf16[576,3072]{1,0:T(8,128)(2,1)} %bitcast.7, bf16[1536,3072]{1,0:T(8,128)(2,1)} %wo_ref.1, bf16[3072,512]{1,0:T(8,128)(2,1)} %wp_ref.1, ...), custom_call_target="tpu_custom_call" | custom-call | tf_op jit(solution)/shard_map/pallas_call | solution.py:558
  148.3 1.9 %copy.9 = bf16[1,24,96,128]{3,2,1,0:T(8,128)(2,1)} copy(bf16[1,24,96,128]{3,2,1,0:T(8,128)(2,1)} %bitcast.8) | data formatting | bytes 1179648

commit v4 on v3

--- a/solution.py
+++ b/solution.py
@@ -31,7 +31,7 @@
 
 
 def body(q_ref, k_ref, v_ref, t_ref, wo_ref, wp_ref, cw_ref, out_ref,
-         win, att, home, res, tok, wo, wp, cw, shard, field, acc, perm4, perm2, back, sent, mid, got, both,
+         win, att, home, res, tok, wo, wp, cw, shard, field, side, acc, perm4, perm2, back, sent, mid, got, both,
          fs, fr, rs, rr, ls, ws, wr, hs, hr, os_, or_, cs, cr):
     r = lax.axis_index("row")
     c = lax.axis_index("col")
@@ -91,6 +91,8 @@
     local[0].start()
     for copy in local[4:]:
         copy.start()
+    for j in (0, 7):
+        field[:, j] = jnp.zeros((8, 16, CH), BF16)
 
     pl.semaphore_wait(barrier, 32 - own_corner.astype(jnp.int32))
 
@@ -270,12 +272,13 @@
             return carry
 
         lax.fori_loop(0, D // CHUNK, chunk, 0)
+        acc[...] += jnp.dot(rows, both[0], preferred_element_type=F32).reshape(6, 6, 16, CH)
 
     last = GROUPS - 2
 
-    def merge():
-        both[...] = jnp.dot(
-            wo[pl.ds(last * WIDE, 2 * WIDE), :], wp[...], preferred_element_type=F32
+    def merge(g, slot):
+        both[slot] = jnp.dot(
+            wo[pl.ds(pl.multiple_of(g * WIDE, WIDE), 2 * WIDE), :], wp[...], preferred_element_type=F32
         ).astype(BF16)
 
     def project():
@@ -283,8 +286,8 @@
 
         def chunk(n, carry):
             rows = pl.ds(pl.multiple_of(n * CHUNK, CHUNK), CHUNK)
-            known = res[:, :, :, lanes(n * CHUNK, CHUNK)].reshape(ROWS, CHUNK).astype(BF16)
-            acc[...] += jnp.dot(known, wp[rows, :], preferred_element_type=F32).reshape(6, 6, 16, CH)
+            own = tok[:, lanes(n * CHUNK, CHUNK)]
+            acc[...] += jnp.dot(own, wp[rows, :], preferred_element_type=F32).reshape(6, 6, 16, CH)
             return carry
 
         lax.fori_loop(0, D // CHUNK, chunk, 0)
@@ -297,23 +300,24 @@
                     send(g, n, t).wait_send()
             send_group(g + WINDOW)
 
-        @pl.when(g == 3)
+        @pl.when(g == 1)
         def _():
             for copy in local[1:4]:
                 copy.wait()
+            project()
+            merge(last, 1)
+
+        @pl.when(jnp.logical_and(g > 1, lax.rem(g, 2) == 0))
+        def _():
+            merge(g - 2, 0)
+
+        @pl.when(g == 3)
+        def _():
             add_pair(0, True)
 
         @pl.when(jnp.logical_and(g > 3, lax.rem(g, 2) == 1))
         def _():
             add_pair(g - 3, False)
-
-        @pl.when(g == GROUPS - 2)
-        def _():
-            merge()
-
-        @pl.when(g == GROUPS - 1)
-        def _():
-            project()
 
         for n in range(3):
             for t in range(3):
@@ -344,91 +348,95 @@
     def rim(i):
         dr, dc = around[i]
         take = [pl.ds(1, 6) if d == 0 else (1 if d < 0 else 6) for d in (dr, dc)]
-        put = [pl.ds(1, 6) if d == 0 else (7 if d < 0 else 0) for d in (dr, dc)]
+        put = pl.ds(1, 6) if dr == 0 else (7 if dr < 0 else 0)
+        there = field.at[put, pl.ds(1, 6)] if dc == 0 else side.at[1 if dc < 0 else 0, put]
         return pltpu.make_async_remote_copy(
-            src_ref=field.at[take[0], take[1]], dst_ref=field.at[put[0], put[1]],
+            src_ref=field.at[take[0], take[1]], dst_ref=there,
             send_sem=hs.at[i], recv_sem=hr.at[i],
             device_id=at(r + dr, c + dc), device_id_type=MESH,
         )
 
-    def columns(ref, spans, span):
-        blocks = [ref[:, pl.ds(j, n), :, span] for j, n in spans]
-        blocks = [block.reshape(-1, block.shape[-1]) for block in blocks]
-        return blocks[0] if len(blocks) == 1 else jnp.concatenate(blocks, axis=0)
-
-    def finish(spans):
-        count = 96 * sum(n for _, n in spans)
-        rows = columns(home, spans, pl.ds(last * WIDE, 2 * WIDE))
+    def cells(ref, blocks, span):
+        taken = [ref[pl.ds(i, m), pl.ds(j, n), :, span] for i, m, j, n in blocks]
+        taken = [block.reshape(-1, block.shape[-1]) for block in taken]
+        return taken[0] if len(taken) == 1 else jnp.concatenate(taken, axis=0)
+
+    def finish(blocks):
+        count = 16 * sum(m * n for _, m, _, n in blocks)
+        rows = cells(home, blocks, pl.ds(last * WIDE, 2 * WIDE))
 
         def chunk(n, squares):
             span = lanes(n * CHUNK, CHUNK)
-            total = columns(res, spans, span) + jnp.dot(
+            total = cells(res, blocks, span) + jnp.dot(
                 rows, wo[pl.ds(last * WIDE, 2 * WIDE), span], preferred_element_type=F32
             )
-            return squares + jnp.sum(total * total, axis=-1, keepdims=True)
-
-        squares = lax.fori_loop(0, D // CHUNK, chunk, jnp.zeros((count, 1), F32))
-        raw = columns(acc, spans, pl.ds(0, CH)) + jnp.dot(rows, both[...], preferred_element_type=F32)
-        raw = raw * lax.rsqrt(squares * (1.0 / D) + 1e-6)
+            for lane in range(0, CHUNK, 128):
+                squares += total[:, lane : lane + 128] * total[:, lane : lane + 128]
+            return squares
+
+        squares = lax.fori_loop(0, D // CHUNK, chunk, jnp.zeros((count, 128), F32))
+        mean = jnp.sum(squares, axis=-1, keepdims=True) * (1.0 / D)
+        raw = cells(acc, blocks, pl.ds(0, CH)) + jnp.dot(rows, both[1], preferred_element_type=F32)
+        raw = raw * lax.rsqrt(mean + 1e-6)
         features = (raw / (1.0 + jnp.exp(-raw))).astype(BF16)
         start = 0
-        for j, n in spans:
-            field[pl.ds(1, 6), pl.ds(1 + j, n)] = features[start : start + 96 * n].reshape(6, n, 16, CH)
-            start += 96 * n
+        for i, m, j, n in blocks:
+            size = 16 * m * n
+            field[pl.ds(1 + i, m), pl.ds(1 + j, n)] = features[start : start + size].reshape(m, n, 16, CH)
+            start += size
 
     sides = (0, 2, 3, 4, 5, 7)
-    finish(((0, 1), (5, 1)))
-    for i in sides:
+    finish(((0, 6, 0, 1), (0, 6, 5, 1), (0, 1, 1, 4), (5, 1, 1, 4)))
+    for i in (1, 6) + sides:
         rim(i).start()
-    finish(((1, 4),))
-    for i in (1, 6):
-        rim(i).start()
+    finish(((1, 4, 1, 4),))
     wait_all(swaps)
-    for i in (1, 6):
-        rim(i).wait()
-
-    @pl.when(r == 0)
-    def _():
-        field[0, pl.ds(1, 6)] = jnp.zeros((6, 16, CH), BF16)
-
-    @pl.when(r == 15)
-    def _():
-        field[7, pl.ds(1, 6)] = jnp.zeros((6, 16, CH), BF16)
-
     def tap_rows(dt, dy, dx):
         return pl.ds(pl.multiple_of(((dt * 3 + dy) * 3 + dx) * CH, CH), CH)
 
-    def centre(dt, carry):
+    def middle(dt, carry):
         total = jnp.zeros((ROWS, CH), F32)
-        for dy in range(3):
+        for dx in range(3):
             total += jnp.dot(
-                field[pl.ds(dy, 6), pl.ds(1, 6)].reshape(ROWS, CH), cw[tap_rows(dt, dy, 1), :],
+                field[pl.ds(1, 6), pl.ds(dx, 6)].reshape(ROWS, CH), cw[tap_rows(dt, 1, dx), :],
                 preferred_element_type=F32,
             )
         res[:, :, :, lanes(dt * 256, 256)] = total[:, :256].reshape(6, 6, 16, 256)
         res[:, :, :, lanes((dt + 3) * 256, 256)] = total[:, 256:].reshape(6, 6, 16, 256)
         return carry
 
-    lax.fori_loop(0, 3, centre, 0)
-
-    for i in sides:
+    lax.fori_loop(0, 3, middle, 0)
+
+    for i in (1, 6):
         rim(i).wait()
 
     @pl.when(r == 0)
     def _():
-        field[0] = jnp.zeros((8, 16, CH), BF16)
+        field[0, pl.ds(1, 6)] = jnp.zeros((6, 16, CH), BF16)
 
     @pl.when(r == 15)
     def _():
-        field[7] = jnp.zeros((8, 16, CH), BF16)
-
-    @pl.when(c == 0)
-    def _():
-        field[:, 0] = jnp.zeros((8, 16, CH), BF16)
-
-    @pl.when(c == 7)
-    def _():
-        field[:, 7] = jnp.zeros((8, 16, CH), BF16)
+        field[7, pl.ds(1, 6)] = jnp.zeros((6, 16, CH), BF16)
+
+    def take_sides():
+        for i in sides:
+            rim(i).wait()
+
+        @pl.when(r == 0)
+        def _():
+            side[:, 0] = jnp.zeros((2, 16, CH), BF16)
+
+        @pl.when(r == 15)
+        def _():
+            side[:, 7] = jnp.zeros((2, 16, CH), BF16)
+
+        @pl.when(c == 0)
+        def _():
+            side[0] = jnp.zeros((8, 16, CH), BF16)
+
+        @pl.when(c == 7)
+        def _():
+            side[1] = jnp.zeros((8, 16, CH), BF16)
 
     def to_y(a, step):
         there = whose_y(step)
@@ -478,8 +486,8 @@
         def tap(dt, carry):
             spot = lanes((a * 3 + dt) * 256, 256)
             total = res[:, :, :, spot].reshape(ROWS, 256)
-            for dy in range(3):
-                for dx in (0, 2):
+            for dy in (0, 2):
+                for dx in range(3):
                     total += jnp.dot(
                         field[pl.ds(dy, 6), pl.ds(dx, 6)].reshape(ROWS, CH),
                         cw[tap_rows(dt, dy, dx), pl.ds(a * 256, 256)],
@@ -489,6 +497,22 @@
             return carry
 
         lax.fori_loop(0, 3, tap, 0)
+        if a == 0:
+            take_sides()
+
+        def edge(dt, carry):
+            spot = lanes((a * 3 + dt) * 256, 256)
+            for e, (j, dx) in enumerate(((0, 0), (5, 2))):
+                total = res[:, j, :, spot].reshape(96, 256)
+                for dy in range(3):
+                    total += jnp.dot(
+                        side[e, pl.ds(dy, 6)].reshape(96, CH), cw[tap_rows(dt, dy, dx), pl.ds(a * 256, 256)],
+                        preferred_element_type=F32,
+                    )
+                res[:, j, :, spot] = total.reshape(6, 16, 256)
+            return carry
+
+        lax.fori_loop(0, 3, edge, 0)
         taps = [res[:, :, :, pl.ds((a * 3 + dt) * 256, 256)].reshape(ROWS, 256) for dt in range(3)]
         conv = taps[2]
         conv += jnp.where(age >= 1, pltpu.roll(taps[1], 1, axis=0), 0.0)
@@ -571,6 +595,7 @@
             pltpu.VMEM((16 * SHARD, CH), BF16),
             pltpu.VMEM((SHARD, CH), BF16),
             pltpu.VMEM((8, 8, 16, CH), BF16),
+            pltpu.VMEM((2, 8, 16, CH), BF16),
             pltpu.VMEM((6, 6, 16, CH), F32),
             pltpu.VMEM((768, 768), BF16),
             pltpu.VMEM((512, 384), BF16),
@@ -578,7 +603,7 @@
             pltpu.VMEM((2, 16, PAD, 128), BF16),
             pltpu.VMEM((2, 4, 4, PAD, 128), BF16),
             pltpu.VMEM((2, 2, 8, PAD, 128), BF16),
-            pltpu.VMEM((2 * WIDE, CH), BF16),
+            pltpu.VMEM((2, 2 * WIDE, CH), BF16),
             dma((GROUPS, 3, 3)), dma((GROUPS, 3, 3)),
             dma((GROUPS, 3)), dma((GROUPS, 4)),
             dma((7,)),

time: 151 us -> 148 us (0.980)
  Pallas kernels: 148 us -> 145 us
    pallas_call x1, Pallas kernels: 148 us -> 145 us  [local(): pl.pallas_call(body, out_shape=jax.ShapeDtypeStruct((24, 96, 128), BF16),...]
where the time goes in v4:
time: 148 us; the launch traced here: 147 us
  Pallas kernels  145 us (98%)
  local copies, waits for them, and re-layouts  1.92 us (1%)
    pallas_call x1, Pallas kernels, local(): pl.pallas_call(body, out_shape=jax.ShapeDtypeStruct((24, 96, 128), BF16),...  145 us

profile of v4, /device:TPU:8, one launch (start us, length us, event | category | flops | bytes accessed | tf_op | source)
XLA Modules:
  0.0 147.0 jit_solution(15910740136000186960)
XLA Ops:
  0.0 145.0 %shard_map.73 = bf16[24,96,128]{2,1,0:T(8,128)(2,1)} custom-call(bf16[6,6,16,1536]{3,2,1,0:T(8,128)(2,1)} %bitcast.9, bf16[6,6,16,1536]{3,2,1,0:T(8,128)(2,1)} %bitcast.10, bf16[6,6,16,1536]{3,2,1,0:T(8,128)(2,1)} %bitcast.11, bf16[576,3072]{1,0:T(8,128)(2,1)} %bitcast.7, bf16[1536,3072]{1,0:T(8,128)(2,1)} %wo_ref.1, bf16[3072,512]{1,0:T(8,128)(2,1)} %wp_ref.1, ...), custom_call_target="tpu_custom_call" | custom-call | tf_op jit(solution)/shard_map/pallas_call | solution.py:582
  145.1 1.9 %copy.9 = bf16[1,24,96,128]{3,2,1,0:T(8,128)(2,1)} copy(bf16[1,24,96,128]{3,2,1,0:T(8,128)(2,1)} %bitcast.8) | data formatting | bytes 1179648

commit v5 on v4

--- a/solution.py
+++ b/solution.py
@@ -366,15 +366,15 @@
         rows = cells(home, blocks, pl.ds(last * WIDE, 2 * WIDE))
 
         def chunk(n, squares):
-            span = lanes(n * CHUNK, CHUNK)
+            span = lanes(n * (2 * CHUNK), (2 * CHUNK))
             total = cells(res, blocks, span) + jnp.dot(
                 rows, wo[pl.ds(last * WIDE, 2 * WIDE), span], preferred_element_type=F32
             )
-            for lane in range(0, CHUNK, 128):
+            for lane in range(0, (2 * CHUNK), 128):
                 squares += total[:, lane : lane + 128] * total[:, lane : lane + 128]
             return squares
 
-        squares = lax.fori_loop(0, D // CHUNK, chunk, jnp.zeros((count, 128), F32))
+        squares = lax.fori_loop(0, D // (2 * CHUNK), chunk, jnp.zeros((count, 128), F32))
         mean = jnp.sum(squares, axis=-1, keepdims=True) * (1.0 / D)
         raw = cells(acc, blocks, pl.ds(0, CH)) + jnp.dot(rows, both[1], preferred_element_type=F32)
         raw = raw * lax.rsqrt(mean + 1e-6)
@@ -386,10 +386,9 @@
             start += size
 
     sides = (0, 2, 3, 4, 5, 7)
-    finish(((0, 6, 0, 1), (0, 6, 5, 1), (0, 1, 1, 4), (5, 1, 1, 4)))
+    finish(((0, 6, 0, 6),))
     for i in (1, 6) + sides:
         rim(i).start()
-    finish(((1, 4, 1, 4),))
     wait_all(swaps)
     def tap_rows(dt, dy, dx):
         return pl.ds(pl.multiple_of(((dt * 3 + dy) * 3 + dx) * CH, CH), CH)

time: 148 us -> 148 us (level)
  no operation moved by 1% of the time
where the time goes in v5:
time: 148 us; the launch traced here: 147 us
  Pallas kernels  145 us (98%)
  local copies, waits for them, and re-layouts  1.92 us (1%)
    pallas_call x1, Pallas kernels, local(): pl.pallas_call(body, out_shape=jax.ShapeDtypeStruct((24, 96, 128), BF16),...  145 us

profile of v5, /device:TPU:8, one launch (start us, length us, event | category | flops | bytes accessed | tf_op | source)
XLA Modules:
  0.0 147.1 jit_solution(12308612266241503408)
XLA Ops:
  0.0 145.2 %shard_map.73 = bf16[24,96,128]{2,1,0:T(8,128)(2,1)} custom-call(bf16[6,6,16,1536]{3,2,1,0:T(8,128)(2,1)} %bitcast.9, bf16[6,6,16,1536]{3,2,1,0:T(8,128)(2,1)} %bitcast.10, bf16[6,6,16,1536]{3,2,1,0:T(8,128)(2,1)} %bitcast.11, bf16[576,3072]{1,0:T(8,128)(2,1)} %bitcast.7, bf16[1536,3072]{1,0:T(8,128)(2,1)} %wo_ref.1, bf16[3072,512]{1,0:T(8,128)(2,1)} %wp_ref.1, ...), custom_call_target="tpu_custom_call" | custom-call | tf_op jit(solution)/shard_map/pallas_call | solution.py:581
  145.2 1.9 %copy.9 = bf16[1,24,96,128]{3,2,1,0:T(8,128)(2,1)} copy(bf16[1,24,96,128]{3,2,1,0:T(8,128)(2,1)} %bitcast.8) | data formatting | bytes 1179648
